TPU v7x, 256 devices: a whole 4x4x8 slice. The times are simulated.
256 devices in a mesh: rep: 4 (over z_lo, core), fsdp: 64 (over x, z_hi, y).
Axes of the slice: x: 4, y: 4, z: 8 (z_hi: 4, z_lo: 2; z = z_hi * 2 + z_lo), core: 2. Of those that a mesh axis runs over, the one named last changes fastest.
Arguments:
- normed: bfloat16 [98304, 4608], P(('rep', 'fsdp')), may hold values from -24 to 24
- key_grad: bfloat16 [98304, 1024], P(('rep', 'fsdp')), may hold values from -6 to 6
- master: float32 [4, 4608, 1024], P('rep', 'fsdp'), may hold values from -6 to 6
- first_moment: float32 [4, 4608, 1024], P('rep', 'fsdp'), may hold values from -6 to 6
- second_moment: float32 [4, 4608, 1024], P('rep', 'fsdp'), may hold values from 0.1 to 10
- anchor: float32 [4608, 1024], P('fsdp'), may hold values from -6 to 6
- momentum: float32 [4608, 1024], P('fsdp'), may hold values from -6 to 6
- inner_step: int32 [1], replicated, may hold values from 1 to 6
Outputs:
- keys: bfloat16 [98304, 1024], P(('rep', 'fsdp'))
- input_grad: bfloat16 [98304, 4608], P(('rep', 'fsdp'))
- merged: float32 [4, 4608, 1024], P('rep', 'fsdp')
- new_first: float32 [4, 4608, 1024], P('rep', 'fsdp')
- new_second: float32 [4, 4608, 1024], P('rep', 'fsdp')
- new_anchor: float32 [4608, 1024], P('fsdp')
- new_momentum: float32 [4608, 1024], P('fsdp')
Inputs may be any that keep to these rules, and one draw needn't show every extreme that they name: `inner_step`: the 1-based count of inner steps taken by the inner optimizer.
All inputs are finite; a program needn't handle non-finite values.
Results may differ from a plain program's by a relative error of at most 0.0049.
Values may be sent and summed in bfloat16 or wider, within the bound.
A program may use at most 128 MiB of HBM per device.

v0:
```python
import jax
import jax.numpy as jnp
from jax import lax
from jax.sharding import PartitionSpec as P

beta_first = 0.9
beta_second = 0.95
inner_rate = 0.1
weight_decay = 0.1
epsilon = 1e-08
outer_rate = 0.7
outer_mu = 0.9
mix_weight = 0.5


def nesterov(outer_grad, anchor_rows, moment_rows):
    moment_new = outer_mu * moment_rows + outer_grad
    anchor_new = anchor_rows - outer_rate * (outer_grad + outer_mu * moment_new)
    return (anchor_new, moment_new)


def outer_update(local, anchor, momentum):
    delta = anchor - local
    replicas = lax.axis_size("rep")
    summed = lax.psum(delta, "rep")
    return nesterov(summed / replicas, anchor, momentum)


def inner_pass(normed, key_grad, local, first_old, second_old, inner_step):
    width = normed.shape[1]
    scale = width ** (-0.5)
    weight_half = local.astype(jnp.bfloat16)
    piece = lax.all_gather(weight_half, "fsdp", axis=0, tiled=True)
    columns = normed
    key_total = jnp.dot(columns, piece, preferred_element_type=jnp.float32)
    block = lax.dot_general(
        key_grad, piece, (((1,), (1,)), ((), ())), preferred_element_type=jnp.float32
    )
    keys = (key_total * scale).astype(jnp.bfloat16)
    input_grad = (block * scale).astype(jnp.bfloat16)
    columns = normed
    gradient = lax.psum_scatter(
        lax.dot_general(
            columns, key_grad, (((0,), (0,)), ((), ())), preferred_element_type=jnp.float32
        )
        * scale,
        "fsdp",
        scatter_dimension=0,
        tiled=True,
    )
    count_float = inner_step[0].astype(jnp.float32)
    fix_first = 1.0 - jnp.power(jnp.float32(beta_first), count_float)
    fix_second = 1.0 - jnp.power(jnp.float32(beta_second), count_float)
    first_new = beta_first * first_old + (1.0 - beta_first) * gradient
    second_new = beta_second * second_old + (1.0 - beta_second) * gradient * gradient
    direction = first_new / fix_first / (jnp.sqrt(second_new / fix_second) + epsilon)
    stepped = local - inner_rate * (direction + weight_decay * local)
    return (keys, input_grad, stepped, first_new, second_new)


def body(normed, key_grad, master, first_moment, second_moment, anchor, momentum, inner_step):
    local = master[0]
    keys, input_grad, stepped, first_new, second_new = inner_pass(
        normed, key_grad, local, first_moment[0], second_moment[0], inner_step
    )
    anchor_new, moment_new = outer_update(local, anchor, momentum)
    merged = mix_weight * stepped + (1.0 - mix_weight) * anchor_new
    return (
        keys,
        input_grad,
        merged[None],
        first_new[None],
        second_new[None],
        anchor_new,
        moment_new,
    )


def solution(mesh):
    in_specs = (
        P(("rep", "fsdp"), None),
        P(("rep", "fsdp"), None),
        P("rep", "fsdp", None),
        P("rep", "fsdp", None),
        P("rep", "fsdp", None),
        P("fsdp", None),
        P("fsdp", None),
        P(),
    )
    out_specs = (
        P(("rep", "fsdp"), None),
        P(("rep", "fsdp"), None),
        P("rep", "fsdp", None),
        P("rep", "fsdp", None),
        P("rep", "fsdp", None),
        P("fsdp", None),
        P("fsdp", None),
    )
    return jax.shard_map(body, mesh=mesh, in_specs=in_specs, out_specs=out_specs, check_vma=False)
```

profile of v0, /device:TPU:6, one launch (start us, length us, event | category | flops | bytes accessed | tf_op | source)
XLA Modules:
  0.0 434.8 jit_solution(15090324106622991514)
XLA Ops:
  8.0 0.0 copy-start
  8.0 0.0 all-gather.2.cloned.1.call-start
  8.1 1.8 bitcast_convert_fusion
  9.9 0.0 all-gather.2.cloned.1.call-update
  9.9 0.0 all-reduce.2.cloned.1.call-start
  9.9 1.8 bitcast_subtract_fusion
  11.7 0.0 all-reduce.2.cloned.1.call-update
  11.8 0.0 reduce-scatter.2.cloned.1.call-start
  11.8 0.0 copy-done
  11.8 10.3 %broadcast_multiply_fusion = f32[4608,1024]{1,0:T(8,128)} fusion(bf16[384,4608]{1,0:T(8,128)(2,1)S(1)} %copy-done, bf16[384,1024]{1,0:T(8,128)(2,1)} %param.9), kind=kOutput, calls=%fused_computation | convolution fusion | flops 3628597248 | bytes 23199744 | tf_op jit(solution)/shard_map/dot_general | solution.py:43
  22.1 0.0 reduce-scatter.2.cloned.1.call-update
  22.8 113.4 %all-gather.2.cloned.1.call-done = bf16[4608,1024]{1,0:T(8,128)(2,1)} async-done(((bf16[72,1024]{1,0:T(8,128)(2,1)}), bf16[4608,1024]{1,0:T(8,128)(2,1)}) %all-gather.2.cloned.1.call-update) | async-done | bytes 9437200 | tf_op jit(solution)/shard_map/all_gather | solution.py:33
  136.2 0.0 copy-start.1
  136.2 9.7 %fusion = bf16[384,4608]{1,0:T(8,128)(2,1)} fusion(bf16[384,1024]{1,0:T(8,128)(2,1)} %param.9, bf16[4608,1024]{1,0:T(8,128)(2,1)} %all-gather.2.cloned.1.call-done), kind=kOutput, calls=%fused_computation.2 | convolution fusion | flops 3627417600 | bytes 13762560 | tf_op jit(solution)/shard_map/dot_general | solution.py:36
  145.9 0.0 copy-done.1
  145.9 4.9 %multiply_convert_fusion = bf16[384,1024]{1,0:T(8,128)(2,1)} fusion(bf16[384,4608]{1,0:T(8,128)(2,1)S(1)} %copy-done, bf16[4608,1024]{1,0:T(8,128)(2,1)S(1)} %copy-done.1), kind=kOutput, calls=%fused_computation.3 | convolution fusion | flops 3624665088 | bytes 13762560 | tf_op jit(solution)/shard_map/dot_general | solution.py:35
  150.8 0.0 all-reduce.2.cloned.1.call-done
  150.9 273.8 %reduce-scatter.2.cloned.1.call-done = f32[72,1024]{1,0:T(8,128)} async-done(((f32[4608,1024]{1,0:T(8,128)}), f32[72,1024]{1,0:T(8,128)}) %reduce-scatter.2.cloned.1.call-update) | async-done | bytes 294928 | tf_op jit(solution)/shard_map/reduce_scatter | solution.py:42
  424.7 2.7 fusion.6
Async XLA Ops:
  8.0 3.8 copy-start
  8.0 128.2 %all-gather.2.cloned.1.call-start = ((), (), s32[]{:S(2)}) async-start(), calls=%async_computation.1 | async-start | bytes 9584640 | tf_op jit(solution)/shard_map/all_gather | solution.py:33
  9.9 141.0 %all-reduce.2.cloned.1.call-start = ((), (), s32[]{:S(2)}) async-start(), calls=%async_computation.3 | async-start | bytes 589824 | tf_op jit(solution)/shard_map/psum | solution.py:25
  11.8 412.9 %reduce-scatter.2.cloned.1.call-start = ((), (), s32[]{:S(2)}) async-start(), calls=%async_computation.2 | async-start | bytes 19169280 | tf_op jit(solution)/shard_map/reduce_scatter | solution.py:42
  136.2 9.7 %copy-start.1 = (bf16[4608,1024]{1,0:T(8,128)(2,1)S(1)}, bf16[4608,1024]{1,0:T(8,128)(2,1)}, u32[]{:S(2)}) copy-start(bf16[4608,1024]{1,0:T(8,128)(2,1)} %all-gather.2.cloned.1.call-done) | copy-start | bytes 28311556
Sparse Core Ops, SparseCore 0:
  12.6 123.5 all-gather.1
  141.4 283.2 reduce-scatter.1
Sparse Core Ops, SparseCore 1:
  13.8 46.6 all-reduce.1
where the time goes:
time: 435 us
  waiting for transfers between devices  387 us (89%)
  matrix products  24.9 us (6%)
  between operations  16.2 us (4%)
  other arithmetic  6.3 us (1%)
    reduce_scatter x1, waiting for transfers between devices, inner_pass(): lax.psum_scatter(lax.dot_general(columns, key_grad, (((0,), (0,)), ((), (...  274 us
    all_gather x1, waiting for transfers between devices, inner_pass(): piece = lax.all_gather(weight_half, 'fsdp', axis=0, tiled=True)  113 us
    dot_general x1, matrix products, inner_pass(): lax.dot_general(columns, key_grad, (((0,), (0,)), ((), ())), preferred_el...  10.3 us
    dot_general x1, matrix products, inner_pass(): lax.dot_general(key_grad, piece, (((1,), (1,)), ((), ())), preferred_elem...  9.72 us
  transfers between devices with their start and end apart: 3, of which 2 were waited for; matrix products, arithmetic and copies ran while one was open for 6% of the time, Pallas kernels for 0%

commit v1 on v0

v1 whole, which is shorter than its diff:
```python
import jax
import jax.numpy as jnp
from jax import lax
from jax.experimental import pallas as pl
from jax.experimental.pallas import tpu as pltpu
from jax.sharding import PartitionSpec as P

beta_first = 0.9
beta_second = 0.95
inner_rate = 0.1
weight_decay = 0.1
epsilon = 1e-08
outer_rate = 0.7
outer_mu = 0.9
mix_weight = 0.5

MESH = pl.DeviceIdType.MESH
D, KD, TOK = 4608, 1024, 384
ROWS = 72
HALF = KD // 2
CHUNK = 4 * ROWS
HROWS = CHUNK // 2
BLOCK = 4 * CHUNK
TO_RIGHT = (2, 0)
TO_LEFT = (1, 3)
F32, BF16 = jnp.float32, jnp.bfloat16


def f32(v):
    return v.astype(F32)


def kernel(
    normed_hbm, kg_hbm, master_hbm, keys_hbm, ig_hbm, grad_hbm,
    xv, kgv, mv, keysv, igv, gradv,
    w, wnat, g, gnat, first_send, first_recv,
    r1, r1x, r2, r2x, third, r3,
    load_sem, store_sem,
    f_send, f_got, a2_send, a2_got, a2x_send, a2x_got,
    a3_send, a3_got, a3x_send, a3x_got,
    s1x_send, s1x_got, s1_send, s1_got,
    s2x_send, s2x_got, s2_send, s2_got, s3_send, s3_got,
):
    rep = lax.axis_index("rep")
    shard = lax.axis_index("fsdp")
    x, z, y = shard // 16, (shard // 4) % 4, shard % 4

    def dev(dx, dz, dy):
        return (rep, ((x + dx) % 4) * 16 + ((z + dz) % 4) * 4 + (y + dy) % 4)

    first_pos, last_pos = (x, y), (y, x)
    first_dev = (lambda d: dev(d, 0, 0), lambda d: dev(0, 0, d))
    last_dev = (first_dev[1], first_dev[0])

    def z_dev(d):
        return dev(0, d, 0)

    pending = []

    def send(src, dst, ssem, rsem, target):
        copy = pltpu.make_async_remote_copy(
            src_ref=src, dst_ref=dst, send_sem=ssem, recv_sem=rsem,
            device_id=target, device_id_type=MESH,
        )
        copy.start()
        pending.append(copy)

    def got(dst, ssem, rsem):
        pltpu.make_async_remote_copy(
            src_ref=dst, dst_ref=dst, send_sem=ssem, recv_sem=rsem,
            device_id=z_dev(1), device_id_type=MESH,
        ).wait_recv()

    loads = [
        pltpu.make_async_copy(master_hbm, mv, load_sem.at[0]),
        pltpu.make_async_copy(normed_hbm, xv, load_sem.at[1]),
        pltpu.make_async_copy(kg_hbm, kgv, load_sem.at[2]),
    ]
    for copy in loads:
        copy.start()

    barrier = pltpu.get_barrier_semaphore()
    peers = [first_dev[s](d) for s in (0, 1) for d in (1, 3, 2)] + [z_dev(1), z_dev(3)]
    for peer in peers:
        pl.semaphore_signal(barrier, inc=1, device_id=peer, device_id_type=MESH)
    pl.semaphore_wait(barrier, len(peers))

    loads[0].wait()
    for s in (0, 1):
        own = mv[:, s * HALF:(s + 1) * HALF]
        packed = jnp.concatenate([own[:, :HALF // 2], own[:, HALF // 2:]], axis=0).astype(BF16)
        first_send[s] = packed
        first_recv[s, first_pos[s]] = packed
        for d in (1, 3, 2):
            send(first_send.at[s], first_recv.at[s, first_pos[s]],
                 f_send.at[s, d], f_got.at[s, d], first_dev[s](d))

    def chunk_at(s, d, k):
        return ((last_pos[s] + d) % 4) * 4 + (z + k) % 4

    def send_relay(s):
        for n, k in enumerate(TO_RIGHT):
            send(g.at[s, chunk_at(s, 2, k)], r1x.at[s, 0, n],
                 s1x_send.at[s, 0, n], s1x_got.at[s, 0, n], last_dev[s](1))
        for n, k in enumerate(TO_LEFT):
            send(g.at[s, chunk_at(s, 2, k)], r1x.at[s, 1, n],
                 s1x_send.at[s, 1, n], s1x_got.at[s, 1, n], last_dev[s](3))

    def send_one(s, way, k):
        send(g.at[s, chunk_at(s, 1 if way == 0 else 3, k)], r1.at[s, way, k],
             s1_send.at[s, way, k], s1_got.at[s, way, k], last_dev[s](1 if way == 0 else 3))

    loads[1].wait()
    loads[2].wait()

    def tn(lhs, rhs):
        return lax.dot_general(lhs, rhs, (((0,), (0,)), ((), ())), preferred_element_type=F32)

    def grad_one(block):
        def step(i, _):
            at = pl.multiple_of(block * BLOCK + i * TOK, 128)
            part = tn(xv[:, pl.ds(at, TOK)], kgv[:, HALF:]).astype(BF16)
            flat = g.at[1, pl.ds(block * 4, 4)]
            for n in range(TOK // 96):
                row = i * TOK + n * 96
                flat[row // CHUNK, pl.ds(pl.multiple_of(row % CHUNK, 96), 96)] = part[n * 96:(n + 1) * 96]
            return 0
        lax.fori_loop(0, BLOCK // TOK, step, 0)

    grad_one((x + 2) % 4)
    send_relay(1)

    def grad_zero(i, _):
        at = pl.multiple_of(i * TOK, 128)
        gnat[pl.ds(at, TOK)] = tn(xv[:, pl.ds(at, TOK)], kgv[:, :HALF])
        return 0
    lax.fori_loop(0, D // TOK, grad_zero, 0)

    def pack(block):
        def step(k, _):
            for half in (0, 1):
                pieces = [
                    gnat[pl.ds(pl.multiple_of(a * BLOCK + k * CHUNK + block * ROWS, 8), ROWS)]
                    for a in (2 * half, 2 * half + 1)
                ]
                g[0, block * 4 + k, half * HROWS:(half + 1) * HROWS] = jnp.concatenate(pieces, axis=0).astype(BF16)
            return 0
        lax.fori_loop(0, 4, step, 0)

    pack((y + 2) % 4)
    send_relay(0)
    for d in (1, 3):
        grad_one((x + d) % 4)
        pack((y + d) % 4)
        for s in (1, 0):
            way = 0 if d == 1 else 1
            for k in (TO_LEFT if d == 1 else TO_RIGHT):
                send_one(s, way, k)
    grad_one(x)
    pack(y)

    def send_second(s, way, h):
        here = w.at[s, last_pos[s] * 4 + z, pl.ds(h * HROWS, HROWS)]
        send(here, here, a2_send.at[s, way, h], a2_got.at[s, way, h], z_dev(1 if way == 0 else 3))

    for s in (0, 1):
        for d in (1, 3, 2):
            got(first_recv.at[s, (first_pos[s] - d) % 4], f_send.at[s, d], f_got.at[s, d])
        pieces = []
        for j in range(4):
            piece = f32(first_recv[s, j])
            pieces.append(jnp.concatenate([piece[:ROWS], piece[ROWS:]], axis=1))
        w[s, last_pos[s] * 4 + z] = jnp.concatenate(pieces, axis=0).astype(BF16)
        send_second(s, 0, 0)
        send_second(s, 1, 1)
    for s in (0, 1):
        send_second(s, 0, 1)
        send_second(s, 1, 0)

    def add_rows(dst, rows, sources):
        def step(i, _):
            at = pl.ds(pl.multiple_of(i * 48, 48), 48)
            total = f32(sources[0][at])
            for ref in sources[1:]:
                total = total + f32(ref[at])
            dst[at] = total.astype(dst.dtype)
            return 0
        lax.fori_loop(0, rows // 48, step, 0)

    def hand_on(n):
        for s in (1, 0):
            for way, k in ((0, TO_RIGHT[n]), (1, TO_LEFT[n])):
                got(r1x.at[s, way, n], s1x_send.at[s, way, n], s1x_got.at[s, way, n])
                here = g.at[s, chunk_at(s, 1 if way == 0 else 3, k)]
                add_rows(here, CHUNK, [here, r1x.at[s, way, n]])
                send_one(s, way, k)

    def second_at(s, d, h):
        return w.at[s, last_pos[s] * 4 + (z + d) % 4, pl.ds(h * HROWS, HROWS)]

    def wait_second(s, way, h):
        got(second_at(s, 3 if way == 0 else 1, h), a2_send.at[s, way, h], a2_got.at[s, way, h])

    hand_on(0)
    for s in (0, 1):
        for way in (0, 1):
            wait_second(s, way, way)
            here = second_at(s, 3 if way == 0 else 1, way)
            send(here, here, a2x_send.at[s, way], a2x_got.at[s, way], z_dev(1 if way == 0 else 3))
    hand_on(1)

    def close(s, k, h, extra=()):
        rows = pl.ds(h * HROWS, HROWS)
        here = g.at[s, chunk_at(s, 0, k), rows]
        add_rows(here, HROWS, [here, r1.at[s, 0, k, rows], r1.at[s, 1, k, rows], *extra])
        return here

    def wait_last(k):
        for s in (0, 1):
            for way in (0, 1):
                got(r1.at[s, way, k], s1_send.at[s, way, k], s1_got.at[s, way, k])

    wait_last(2)
    for s in (0, 1):
        for way in (0, 1):
            send(close(s, 2, way), r2x.at[s, way], s2x_send.at[s, way], s2x_got.at[s, way],
                 z_dev(1 if way == 0 else 3))

    def send_third(s, way, k):
        here = w.at[s, chunk_at(s, 0, k)]
        send(here, here, a3_send.at[s, way, k], a3_got.at[s, way, k], last_dev[s](1 if way == 0 else 3))

    def hand_third(s, way, k):
        here = w.at[s, chunk_at(s, 3 if way == 0 else 1, k)]
        got(here, a3_send.at[s, way, k], a3_got.at[s, way, k])
        send(here, here, a3x_send.at[s, k], a3x_got.at[s, k], last_dev[s](1 if way == 0 else 3))

    for s in (0, 1):
        for way in (0, 1):
            send_third(s, way, 0)

    def send_plain_z(s, way):
        k, h = (1, 1) if way == 0 else (3, 0)
        send(close(s, k, h), r2.at[s, way, h], s2_send.at[s, way, h], s2_got.at[s, way, h],
             z_dev(1 if way == 0 else 3))

    wait_last(1)
    for s in (0, 1):
        send_plain_z(s, 0)
    wait_last(3)
    for s in (0, 1):
        send_plain_z(s, 1)

    for s in (0, 1):
        for way in (0, 1):
            wait_second(s, way, 1 - way)
    for k in (1, 3):
        for s in (0, 1):
            for way in (0, 1):
                send_third(s, way, k)
    for s in (0, 1):
        for way in (0, 1):
            got(second_at(s, 2, way), a2x_send.at[s, way], a2x_got.at[s, way])
    for s in (0, 1):
        for way in (0, 1):
            send_third(s, way, 2)

    for s in (0, 1):
        for way in (0, 1):
            got(r2x.at[s, way], s2x_send.at[s, way], s2x_got.at[s, way])
            k, h = (1, 0) if way == 0 else (3, 1)
            send(close(s, k, h, (r2x.at[s, way],)), r2.at[s, way, h],
                 s2_send.at[s, way, h], s2_got.at[s, way, h], z_dev(1 if way == 0 else 3))

    for n in (1, 0):
        for s in (0, 1):
            hand_third(s, 0, TO_RIGHT[n])
            hand_third(s, 1, TO_LEFT[1 - n])

    wait_last(0)
    for s in (0, 1):
        for h in (0, 1):
            for way in (0, 1):
                got(r2.at[s, way, h], s2_send.at[s, way, h], s2_got.at[s, way, h])
            rows = pl.ds(h * HROWS, HROWS)
            add_rows(third.at[s, rows], HROWS,
                     [g.at[s, chunk_at(s, 0, 0), rows], r1.at[s, 0, 0, rows], r1.at[s, 1, 0, rows],
                      r2.at[s, 0, h], r2.at[s, 1, h]])
        for d in (2, 1, 3):
            at = pl.multiple_of(((first_pos[s] + d) % 4) * ROWS, 8)
            send(third.at[s, pl.ds(at, ROWS)], r3.at[s, d], s3_send.at[s, d], s3_got.at[s, d], first_dev[s](d))

    for s in (0, 1):
        for way, ks in ((0, TO_LEFT), (1, TO_RIGHT)):
            for k in ks:
                got(w.at[s, chunk_at(s, 3 if way == 0 else 1, k)], a3_send.at[s, way, k], a3_got.at[s, way, k])
        for k in range(4):
            got(w.at[s, chunk_at(s, 2, k)], a3x_send.at[s, k], a3x_got.at[s, k])

    def unpack(k, _):
        for a in range(4):
            low = a * ROWS - 8 * (a % 2)
            pieces = []
            for b in range(4):
                piece = f32(w[0, b * 4 + k, low:low + ROWS + 8])
                skip = 8 * (a % 2)
                pieces.append(piece[skip:skip + ROWS])
            wnat[a * 4 + k] = jnp.concatenate(pieces, axis=0).astype(BF16)
        return 0
    lax.fori_loop(0, 4, unpack, 0)

    scale = D ** (-0.5)

    def nt(lhs, rhs):
        return lax.dot_general(lhs, rhs, (((1,), (1,)), ((), ())), preferred_element_type=F32)

    def weight(ref, b):
        return ref[pl.ds(b * 4, 4)].reshape(BLOCK, HALF)

    def back(b, _):
        at = pl.multiple_of(b * BLOCK, 128)
        part = nt(kgv[:, :HALF], weight(wnat, b)) + nt(kgv[:, HALF:], weight(w.at[1], b))
        igv[:, pl.ds(at, BLOCK)] = (part * scale).astype(BF16)
        return 0
    lax.fori_loop(0, 4, back, 0)
    store_ig = pltpu.make_async_copy(igv, ig_hbm, store_sem.at[0])
    store_ig.start()
    for s, ref in ((0, wnat), (1, w.at[1])):
        total = None
        for b in range(4):
            part = jnp.dot(xv[:, b * BLOCK:(b + 1) * BLOCK], weight(ref, b), preferred_element_type=F32)
            total = part if total is None else total + part
        keysv[:, s * HALF:(s + 1) * HALF] = (total * scale).astype(BF16)
    store_keys = pltpu.make_async_copy(keysv, keys_hbm, store_sem.at[1])
    store_keys.start()

    for s in (0, 1):
        at = pl.multiple_of(first_pos[s] * ROWS, 8)
        total = third[s, pl.ds(at, ROWS)]
        for d in (1, 3, 2):
            got(r3.at[s, d], s3_send.at[s, d], s3_got.at[s, d])
            total = total + r3[s, d]
        gradv[:, s * HALF:(s + 1) * HALF] = total * scale
    store_grad = pltpu.make_async_copy(gradv, grad_hbm, store_sem.at[2])
    store_grad.start()

    for copy in pending:
        copy.wait_send()
    store_ig.wait()
    store_keys.wait()
    store_grad.wait()


def exchange(normed, key_grad, local):
    any_space = pl.BlockSpec(memory_space=pl.ANY)
    dma = pltpu.SemaphoreType.DMA
    return pl.pallas_call(
        kernel,
        out_shape=(
            jax.ShapeDtypeStruct((TOK, KD), BF16),
            jax.ShapeDtypeStruct((TOK, D), BF16),
            jax.ShapeDtypeStruct((ROWS, KD), F32),
        ),
        in_specs=[any_space] * 3,
        out_specs=(any_space,) * 3,
        scratch_shapes=[
            pltpu.VMEM((TOK, D), BF16),
            pltpu.VMEM((TOK, KD), BF16),
            pltpu.VMEM((ROWS, KD), F32),
            pltpu.VMEM((TOK, KD), BF16),
            pltpu.VMEM((TOK, D), BF16),
            pltpu.VMEM((ROWS, KD), F32),
            pltpu.VMEM((2, 16, CHUNK, HALF), BF16),
            pltpu.VMEM((16, CHUNK, HALF), BF16),
            pltpu.VMEM((2, 16, CHUNK, HALF), BF16),
            pltpu.VMEM((D, HALF), F32),
            pltpu.VMEM((2, 2 * ROWS, HALF // 2), BF16),
            pltpu.VMEM((2, 4, 2 * ROWS, HALF // 2), BF16),
            pltpu.VMEM((2, 2, 4, CHUNK, HALF), BF16),
            pltpu.VMEM((2, 2, 2, CHUNK, HALF), BF16),
            pltpu.VMEM((2, 2, 2, HROWS, HALF), BF16),
            pltpu.VMEM((2, 2, HROWS, HALF), BF16),
            pltpu.VMEM((2, CHUNK, HALF), F32),
            pltpu.VMEM((2, 4, ROWS, HALF), F32),
            dma((3,)), dma((3,)),
            dma((2, 4)), dma((2, 4)),
            dma((2, 2, 2)), dma((2, 2, 2)), dma((2, 2)), dma((2, 2)),
            dma((2, 2, 4)), dma((2, 2, 4)), dma((2, 4)), dma((2, 4)),
            dma((2, 2, 2)), dma((2, 2, 2)), dma((2, 2, 4)), dma((2, 2, 4)),
            dma((2, 2)), dma((2, 2)), dma((2, 2, 2)), dma((2, 2, 2)), dma((2, 4)), dma((2, 4)),
        ],
        compiler_params=pltpu.CompilerParams(
            collective_id=0, has_side_effects=True, vmem_limit_bytes=60 * 2**20
        ),
        cost_estimate=pl.CostEstimate(
            flops=6 * TOK * D * KD, bytes_accessed=10 * 2**20, transcendentals=0
        ),
        name="exchange",
    )(normed, key_grad, local)


def nesterov(outer_grad, anchor_rows, moment_rows):
    moment_new = outer_mu * moment_rows + outer_grad
    anchor_new = anchor_rows - outer_rate * (outer_grad + outer_mu * moment_new)
    return (anchor_new, moment_new)


def body(normed, key_grad, master, first_moment, second_moment, anchor, momentum, inner_step):
    local, first_old, second_old = master[0], first_moment[0], second_moment[0]
    summed = lax.psum(anchor - local, "rep")
    keys, input_grad, gradient = exchange(normed, key_grad, local)
    anchor_new, moment_new = nesterov(summed / lax.axis_size("rep"), anchor, momentum)
    count_float = inner_step[0].astype(F32)
    fix_first = 1.0 - jnp.power(F32(beta_first), count_float)
    fix_second = 1.0 - jnp.power(F32(beta_second), count_float)
    first_new = beta_first * first_old + (1.0 - beta_first) * gradient
    second_new = beta_second * second_old + (1.0 - beta_second) * gradient * gradient
    direction = first_new / fix_first / (jnp.sqrt(second_new / fix_second) + epsilon)
    stepped = local - inner_rate * (direction + weight_decay * local)
    merged = mix_weight * stepped + (1.0 - mix_weight) * anchor_new
    return (
        keys,
        input_grad,
        merged[None],
        first_new[None],
        second_new[None],
        anchor_new,
        moment_new,
    )


def solution(mesh):
    in_specs = (
        P(("rep", "fsdp"), None),
        P(("rep", "fsdp"), None),
        P("rep", "fsdp", None),
        P("rep", "fsdp", None),
        P("rep", "fsdp", None),
        P("fsdp", None),
        P("fsdp", None),
        P(),
    )
    out_specs = (
        P(("rep", "fsdp"), None),
        P(("rep", "fsdp"), None),
        P("rep", "fsdp", None),
        P("rep", "fsdp", None),
        P("rep", "fsdp", None),
        P("fsdp", None),
        P("fsdp", None),
    )
    return jax.shard_map(body, mesh=mesh, in_specs=in_specs, out_specs=out_specs, check_vma=False)
```

time: 435 us -> 144 us (0.33)
  waiting for transfers between devices: 387 us -> 0.04 us
  Pallas kernels: 0 us -> 118 us
  matrix products: 24.9 us -> 0 us
    reduce_scatter x1 -> x0, waiting for transfers between devices: 274 us -> none  [inner_pass(): lax.psum_scatter(lax.dot_general(columns, key_grad, (((0,), (0,)), ((), (...]
    pallas_call x0 -> x1, Pallas kernels: none -> 118 us  [exchange(): pl.pallas_call(kernel, out_shape=(jax.ShapeDtypeStruct((TOK, KD), BF16),...]
    all_gather x1 -> x0, waiting for transfers between devices: 113 us -> none  [inner_pass(): piece = lax.all_gather(weight_half, 'fsdp', axis=0, tiled=True)]
    dot_general x3 -> x0, matrix products: 24.9 us -> none  [the longest x1 10.3 us: inner_pass(): lax.dot_general(columns, key_grad, (((0,), (0,)), ((), ())), preferred_el...]
  transfers between devices with their start and end apart: 3 -> 1, of which waited for: 2 -> 0; matrix products, arithmetic and copies ran while one was open for 6% -> 0% of each run, Pallas kernels for 0% -> 83%
where the time goes in v1:
time: 144 us; the launch traced here: 141 us
  Pallas kernels  118 us (82%)
  between operations  14.9 us (10%)
  other arithmetic  4.66 us (3%)
  local copies, waits for them, and re-layouts  3.86 us (3%)
    pallas_call x1, Pallas kernels, exchange(): pl.pallas_call(kernel, out_shape=(jax.ShapeDtypeStruct((TOK, KD), BF16),...  118 us
    unnamed x4, local copies, waits for them, and re-layouts  3.86 us
  transfers between devices with their start and end apart: 1, of which 0 were waited for; matrix products, arithmetic and copies ran while one was open for 0% of the time, Pallas kernels for 83%

profile of v1, /device:TPU:6, one launch (start us, length us, event | category | flops | bytes accessed | tf_op | source)
XLA Modules:
  0.0 141.4 jit_solution(18003078982886170250)
XLA Ops:
  7.2 0.0 all-reduce.2.cloned.1.call-start
  7.2 1.8 %bitcast_subtract_fusion = f32[72,1024]{1,0:T(8,128)} fusion(f32[72,1024]{1,0:T(8,128)} %param.13, f32[1,72,1024]{2,1,0:T(8,128)} %param.10), kind=kLoop, calls=%fused_computation.8 | loop fusion | flops 73728 | bytes 884736 | tf_op jit(solution)/shard_map/sub | solution.py:410
  9.0 0.0 all-reduce.2.cloned.1.call-update
  9.0 117.9 %exchange.1 = (bf16[384,1024]{1,0:T(8,128)(2,1)}, bf16[384,4608]{1,0:T(8,128)(2,1)}, f32[72,1024]{1,0:T(8,128)}) custom-call(bf16[384,4608]{1,0:T(8,128)(2,1)} %normed_hbm.1, bf16[384,1024]{1,0:T(8,128)(2,1)} %kg_hbm.1, f32[72,1024]{1,0:T(8,128)} %bitcast.23), custom_call_target="tpu_custom_call" | custom-call | flops 10871635968 | bytes 10485760 | tf_op jit(solution)/shard_map/exchange/pallas_call | solution.py:357
  126.9 0.0 copy-start
  127.8 0.0 all-reduce.2.cloned.1.call-done
  127.8 2.9 %multiply_bitcast_fusion = (f32[1,72,1024]{2,1,0:T(8,128)}, f32[72,1024]{1,0:T(8,128)}, f32[72,1024]{1,0:T(8,128)}, f32[1,72,1024]{2,1,0:T(8,128)}, f32[1,72,1024]{2,1,0:T(8,128)}) fusion(f32[]{:T(128)} %bitcast.4, f32[]{:T(128)} %bitcast.2, f32[72,1024]{1,0:T(8,128)} %get-tuple-element.12, f32[1,72,1024]{2,1,0:T(8,128)} %param.11, f32[1,72,1024]{2,1,0:T(8,128)} %param.12, ...), kind=kLoop, calls=%fused_computation.3 | loop fusion | flops 1769472 | bytes 3538952 | tf_op jit(solution)/shard_map/broadcast_in_dim | solution.py:424
  130.7 2.1 %copy.19 = bf16[384,1024]{1,0:T(8,128)(2,1)} copy(bf16[384,1024]{1,0:T(8,128)(2,1)} %get-tuple-element.25) | data formatting | bytes 1572864
  132.8 0.0 copy-done
  132.8 1.8 %copy.20 = bf16[384,4608]{1,0:T(8,128)(2,1)} copy(bf16[384,4608]{1,0:T(8,128)(2,1)S(1)} %copy-done) | data formatting | bytes 7077888
Async XLA Ops:
  7.2 120.7 %all-reduce.2.cloned.1.call-start = ((), (), s32[]{:S(2)}) async-start(), calls=%async_computation | async-start | bytes 589824 | tf_op jit(solution)/shard_map/psum | solution.py:410
  126.9 5.8 %copy-start = (bf16[384,4608]{1,0:T(8,128)(2,1)S(1)}, bf16[384,4608]{1,0:T(8,128)(2,1)}, u32[]{:S(2)}) copy-start(bf16[384,4608]{1,0:T(8,128)(2,1)} %get-tuple-element.26) | copy-start | bytes 10616836
Sparse Core Ops, SparseCore 0:
  11.2 77.5 all-reduce.1

commit v2 on v1

--- a/solution.py
+++ b/solution.py
@@ -1,3 +1,5 @@
+import math
+
 import jax
 import jax.numpy as jnp
 from jax import lax
@@ -31,11 +33,12 @@
 
 
 def kernel(
-    normed_hbm, kg_hbm, master_hbm, keys_hbm, ig_hbm, grad_hbm,
-    xv, kgv, mv, keysv, igv, gradv,
-    w, wnat, g, gnat, first_send, first_recv,
+    step_ref, normed_hbm, kg_hbm, master_hbm, moment1_hbm, moment2_hbm, anchor_hbm, momentum_hbm,
+    keysv, igv, merged_ref, first_ref, second_ref, anchor_ref, momentum_ref,
+    xv, kgv, mv, m1v, m2v, av, ov, delta, core_got, half_sum, z_got, half_got,
+    w, g, gnat, first_send, first_recv,
     r1, r1x, r2, r2x, third, r3,
-    load_sem, store_sem,
+    load_sem, o_send, o_got,
     f_send, f_got, a2_send, a2_got, a2x_send, a2x_got,
     a3_send, a3_got, a3x_send, a3x_got,
     s1x_send, s1x_got, s1_send, s1_got,
@@ -55,6 +58,10 @@
     def z_dev(d):
         return dev(0, d, 0)
 
+    core = rep % 2
+    core_dev = (rep + 1 - 2 * core, shard)
+    pair_dev = ((rep + 2) % 4, shard)
+
     pending = []
 
     def send(src, dst, ssem, rsem, target):
@@ -75,12 +82,16 @@
         pltpu.make_async_copy(master_hbm, mv, load_sem.at[0]),
         pltpu.make_async_copy(normed_hbm, xv, load_sem.at[1]),
         pltpu.make_async_copy(kg_hbm, kgv, load_sem.at[2]),
+        pltpu.make_async_copy(anchor_hbm, av, load_sem.at[3]),
+        pltpu.make_async_copy(moment1_hbm, m1v, load_sem.at[4]),
+        pltpu.make_async_copy(moment2_hbm, m2v, load_sem.at[5]),
+        pltpu.make_async_copy(momentum_hbm, ov, load_sem.at[6]),
     ]
     for copy in loads:
         copy.start()
 
     barrier = pltpu.get_barrier_semaphore()
-    peers = [first_dev[s](d) for s in (0, 1) for d in (1, 3, 2)] + [z_dev(1), z_dev(3)]
+    peers = [first_dev[s](d) for s in (0, 1) for d in (1, 3, 2)] + [z_dev(1), z_dev(3), core_dev, pair_dev]
     for peer in peers:
         pl.semaphore_signal(barrier, inc=1, device_id=peer, device_id_type=MESH)
     pl.semaphore_wait(barrier, len(peers))
@@ -94,6 +105,10 @@
         for d in (1, 3, 2):
             send(first_send.at[s], first_recv.at[s, first_pos[s]],
                  f_send.at[s, d], f_got.at[s, d], first_dev[s](d))
+
+    loads[3].wait()
+    delta[...] = av[...] - mv[...]
+    send(delta, core_got, o_send.at[0], o_got.at[0], core_dev)
 
     def chunk_at(s, d, k):
         return ((last_pos[s] + d) % 4) * 4 + (z + k) % 4
@@ -129,6 +144,11 @@
 
     grad_one((x + 2) % 4)
     send_relay(1)
+
+    got(core_got, o_send.at[0], o_got.at[0])
+    mine = pl.ds(pl.multiple_of(core * HALF, 128), HALF)
+    half_sum[...] = delta[:, mine] + core_got[:, mine]
+    send(half_sum, z_got, o_send.at[1], o_got.at[1], pair_dev)
 
     def grad_zero(i, _):
         at = pl.multiple_of(i * TOK, 128)
@@ -201,6 +221,10 @@
     def wait_second(s, way, h):
         got(second_at(s, 3 if way == 0 else 1, h), a2_send.at[s, way, h], a2_got.at[s, way, h])
 
+    got(z_got, o_send.at[1], o_got.at[1])
+    z_got[...] = half_sum[...] + z_got[...]
+    send(z_got, half_got.at[:, mine], o_send.at[2], o_got.at[2], core_dev)
+
     hand_on(0)
     for s in (0, 1):
         for way in (0, 1):
@@ -296,6 +320,11 @@
                 got(w.at[s, chunk_at(s, 3 if way == 0 else 1, k)], a3_send.at[s, way, k], a3_got.at[s, way, k])
         for k in range(4):
             got(w.at[s, chunk_at(s, 2, k)], a3x_send.at[s, k], a3x_got.at[s, k])
+
+    for copy in pending:
+        copy.wait_send()
+    pending.clear()
+    wnat = g.at[0]
 
     def unpack(k, _):
         for a in range(4):
@@ -323,55 +352,73 @@
         igv[:, pl.ds(at, BLOCK)] = (part * scale).astype(BF16)
         return 0
     lax.fori_loop(0, 4, back, 0)
-    store_ig = pltpu.make_async_copy(igv, ig_hbm, store_sem.at[0])
-    store_ig.start()
     for s, ref in ((0, wnat), (1, w.at[1])):
         total = None
         for b in range(4):
             part = jnp.dot(xv[:, b * BLOCK:(b + 1) * BLOCK], weight(ref, b), preferred_element_type=F32)
             total = part if total is None else total + part
         keysv[:, s * HALF:(s + 1) * HALF] = (total * scale).astype(BF16)
-    store_keys = pltpu.make_async_copy(keysv, keys_hbm, store_sem.at[1])
-    store_keys.start()
-
+
+    for copy in loads[4:]:
+        copy.wait()
+    other = pl.ds(pl.multiple_of((1 - core) * HALF, 128), HALF)
+    got(half_got.at[:, other], o_send.at[2], o_got.at[2])
+    half_got[:, mine] = z_got[...]
+    outer_grad = half_got[...] * (1.0 / lax.axis_size("rep"))
+    momentum_new = outer_mu * ov[...] + outer_grad
+    anchor_new = av[...] - outer_rate * (outer_grad + outer_mu * momentum_new)
+    momentum_ref[...] = momentum_new
+    anchor_ref[...] = anchor_new
+
+    count = jnp.full((1, HALF), step_ref[0].astype(F32), F32)
+    fix_first = 1.0 / (1.0 - jnp.exp(count * math.log(beta_first)))
+    fix_second = 1.0 / (1.0 - jnp.exp(count * math.log(beta_second)))
     for s in (0, 1):
         at = pl.multiple_of(first_pos[s] * ROWS, 8)
         total = third[s, pl.ds(at, ROWS)]
         for d in (1, 3, 2):
             got(r3.at[s, d], s3_send.at[s, d], s3_got.at[s, d])
             total = total + r3[s, d]
-        gradv[:, s * HALF:(s + 1) * HALF] = total * scale
-    store_grad = pltpu.make_async_copy(gradv, grad_hbm, store_sem.at[2])
-    store_grad.start()
+        gradient = total * scale
+        cols = slice(s * HALF, (s + 1) * HALF)
+        first_new = beta_first * m1v[:, cols] + (1.0 - beta_first) * gradient
+        second_new = beta_second * m2v[:, cols] + (1.0 - beta_second) * gradient * gradient
+        direction = first_new * fix_first / (jnp.sqrt(second_new * fix_second) + epsilon)
+        local = mv[:, cols]
+        stepped = local - inner_rate * (direction + weight_decay * local)
+        first_ref[:, cols] = first_new
+        second_ref[:, cols] = second_new
+        merged_ref[:, cols] = mix_weight * stepped + (1.0 - mix_weight) * anchor_ref[:, cols]
 
     for copy in pending:
         copy.wait_send()
-    store_ig.wait()
-    store_keys.wait()
-    store_grad.wait()
-
-
-def exchange(normed, key_grad, local):
-    any_space = pl.BlockSpec(memory_space=pl.ANY)
+
+
+def exchange(inner_step, *arrays):
     dma = pltpu.SemaphoreType.DMA
+    rows = (ROWS, KD)
     return pl.pallas_call(
         kernel,
         out_shape=(
-            jax.ShapeDtypeStruct((TOK, KD), BF16),
-            jax.ShapeDtypeStruct((TOK, D), BF16),
-            jax.ShapeDtypeStruct((ROWS, KD), F32),
-        ),
-        in_specs=[any_space] * 3,
-        out_specs=(any_space,) * 3,
+            pltpu.VMEM((TOK, KD), BF16),
+            pltpu.VMEM((TOK, D), BF16),
+        ) + (pltpu.VMEM(rows, F32),) * 5,
+        in_specs=[pl.BlockSpec(memory_space=pltpu.SMEM)] + [pl.BlockSpec(memory_space=pl.ANY)] * 7,
+        out_specs=(pl.BlockSpec(memory_space=pltpu.VMEM),) * 7,
         scratch_shapes=[
             pltpu.VMEM((TOK, D), BF16),
             pltpu.VMEM((TOK, KD), BF16),
-            pltpu.VMEM((ROWS, KD), F32),
-            pltpu.VMEM((TOK, KD), BF16),
-            pltpu.VMEM((TOK, D), BF16),
-            pltpu.VMEM((ROWS, KD), F32),
+            pltpu.VMEM(rows, F32),
+            pltpu.VMEM(rows, F32),
+            pltpu.VMEM(rows, F32),
+            pltpu.VMEM(rows, F32),
+            pltpu.VMEM(rows, F32),
+            pltpu.VMEM(rows, F32),
+            pltpu.VMEM(rows, F32),
+            pltpu.VMEM((ROWS, HALF), F32),
+            pltpu.VMEM((ROWS, HALF), F32),
+            pltpu.VMEM(rows, F32),
             pltpu.VMEM((2, 16, CHUNK, HALF), BF16),
-            pltpu.VMEM((16, CHUNK, HALF), BF16),
             pltpu.VMEM((2, 16, CHUNK, HALF), BF16),
             pltpu.VMEM((D, HALF), F32),
             pltpu.VMEM((2, 2 * ROWS, HALF // 2), BF16),
@@ -382,7 +429,7 @@
             pltpu.VMEM((2, 2, HROWS, HALF), BF16),
             pltpu.VMEM((2, CHUNK, HALF), F32),
             pltpu.VMEM((2, 4, ROWS, HALF), F32),
-            dma((3,)), dma((3,)),
+            dma((7,)), dma((3,)), dma((3,)),
             dma((2, 4)), dma((2, 4)),
             dma((2, 2, 2)), dma((2, 2, 2)), dma((2, 2)), dma((2, 2)),
             dma((2, 2, 4)), dma((2, 2, 4)), dma((2, 4)), dma((2, 4)),
@@ -390,34 +437,42 @@
             dma((2, 2)), dma((2, 2)), dma((2, 2, 2)), dma((2, 2, 2)), dma((2, 4)), dma((2, 4)),
         ],
         compiler_params=pltpu.CompilerParams(
-            collective_id=0, has_side_effects=True, vmem_limit_bytes=60 * 2**20
+            collective_id=0, has_side_effects=True, vmem_limit_bytes=48 * 2**20
         ),
         cost_estimate=pl.CostEstimate(
             flops=6 * TOK * D * KD, bytes_accessed=10 * 2**20, transcendentals=0
         ),
         name="exchange",
-    )(normed, key_grad, local)
-
-
-def nesterov(outer_grad, anchor_rows, moment_rows):
-    moment_new = outer_mu * moment_rows + outer_grad
-    anchor_new = anchor_rows - outer_rate * (outer_grad + outer_mu * moment_new)
-    return (anchor_new, moment_new)
+    )(inner_step, *arrays)
+
+
+def store_kernel(*refs):
+    n = len(refs) // 2
+    copies = [pltpu.make_async_copy(refs[i], refs[n + i], refs[-1].at[i]) for i in range(n)]
+    for copy in copies:
+        copy.start()
+    for copy in copies:
+        copy.wait()
+
+
+def store(arrays):
+    any_space = pl.BlockSpec(memory_space=pl.ANY)
+    return pl.pallas_call(
+        store_kernel,
+        out_shape=tuple(jax.ShapeDtypeStruct(a.shape, a.dtype) for a in arrays),
+        in_specs=[pl.BlockSpec(memory_space=pltpu.VMEM)] * len(arrays),
+        out_specs=(any_space,) * len(arrays),
+        scratch_shapes=[pltpu.SemaphoreType.DMA((len(arrays),))],
+        compiler_params=pltpu.CompilerParams(vmem_limit_bytes=2**20),
+        name="store",
+    )(*[pltpu.with_memory_space_constraint(a, pltpu.VMEM) for a in arrays])
 
 
 def body(normed, key_grad, master, first_moment, second_moment, anchor, momentum, inner_step):
-    local, first_old, second_old = master[0], first_moment[0], second_moment[0]
-    summed = lax.psum(anchor - local, "rep")
-    keys, input_grad, gradient = exchange(normed, key_grad, local)
-    anchor_new, moment_new = nesterov(summed / lax.axis_size("rep"), anchor, momentum)
-    count_float = inner_step[0].astype(F32)
-    fix_first = 1.0 - jnp.power(F32(beta_first), count_float)
-    fix_second = 1.0 - jnp.power(F32(beta_second), count_float)
-    first_new = beta_first * first_old + (1.0 - beta_first) * gradient
-    second_new = beta_second * second_old + (1.0 - beta_second) * gradient * gradient
-    direction = first_new / fix_first / (jnp.sqrt(second_new / fix_second) + epsilon)
-    stepped = local - inner_rate * (direction + weight_decay * local)
-    merged = mix_weight * stepped + (1.0 - mix_weight) * anchor_new
+    results = exchange(
+        inner_step, normed, key_grad, master[0], first_moment[0], second_moment[0], anchor, momentum
+    )
+    keys, input_grad, merged, first_new, second_new, anchor_new, momentum_new = store(results)
     return (
         keys,
         input_grad,
@@ -425,7 +480,7 @@
         first_new[None],
         second_new[None],
         anchor_new,
-        moment_new,
+        momentum_new,
     )
 
 

time: 144 us -> 121 us (0.84); the launches traced: 141 us -> 121 us
  between operations: 14.9 us -> 1.3 us
  other arithmetic: 4.66 us -> 0 us
  local copies, waits for them, and re-layouts: 3.86 us -> 0.95 us
    unnamed x4 -> x2, local copies, waits for them, and re-layouts: 3.86 us -> 0.95 us
    broadcast_in_dim x1 -> x0, other arithmetic: 2.86 us -> none  [body(): merged[None]]
    sub x1 -> x0, other arithmetic: 1.8 us -> none  [body(): summed = lax.psum(anchor - local, 'rep')]
    pallas_call x1 -> x2, Pallas kernels: 118 us -> 118 us  [the longest x1 116 us: exchange(): pl.pallas_call(kernel, out_shape=(pltpu.VMEM((TOK, KD), BF16), pltpu.VMEM...]
  transfers between devices with their start and end apart: 1 -> 0, of which waited for: 0 -> 0; matrix products, arithmetic and copies ran while one was open for 0% -> 0% of each run, Pallas kernels for 83% -> 0%
where the time goes in v2:
time: 121 us
  Pallas kernels  118 us (98%)
  between operations  1.3 us (1%)
    pallas_call x1, Pallas kernels, exchange(): pl.pallas_call(kernel, out_shape=(pltpu.VMEM((TOK, KD), BF16), pltpu.VMEM...  116 us
    pallas_call x1, Pallas kernels, store(): pl.pallas_call(store_kernel, out_shape=tuple((jax.ShapeDtypeStruct(a.shap...  2.56 us

profile of v2, /device:TPU:6, one launch (start us, length us, event | category | flops | bytes accessed | tf_op | source)
XLA Modules:
  0.0 120.6 jit_solution(6144160376839444001)
XLA Ops:
  1.3 0.0 copy-start
  1.3 1.0 copy-done
  2.2 115.8 %exchange.1 = (bf16[384,1024]{1,0:T(8,128)(2,1)S(1)}, bf16[384,4608]{1,0:T(8,128)(2,1)S(1)}, f32[72,1024]{1,0:T(8,128)S(1)}, f32[72,1024]{1,0:T(8,128)S(1)}, f32...) custom-call(s32[1]{0:T(128)S(6)} %copy.15.step_ref, bf16[384,4608]{1,0:T(8,128)(2,1)} %normed_hbm.1, ...), custom_call_target="tpu_custom_call" | custom-call | flops 10871635968 | bytes 10485760 | tf_op jit(solution)/shard_map/exchange/pallas_call | solution.py:400
  118.1 2.6 %store.1 = (bf16[384,1024]{1,0:T(8,128)(2,1)}, bf16[384,4608]{1,0:T(8,128)(2,1)}, f32[72,1024]{1,0:T(8,128)}, f32[72,1024]{1,0:T(8,128)}, f32[72,1024]{1,0:T(8,1...) custom-call(bf16[384,1024]{1,0:T(8,128)(2,1)S(1)} %get-tuple-element.21.refs_0_, ...), custom_call_target="tpu_custom_call" | custom-call | tf_op jit(solution)/shard_map/store/pallas_call | solution.py:460
Async XLA Ops:
  1.3 1.0 copy-start

commit v3 on v2

--- a/solution.py
+++ b/solution.py
@@ -33,11 +33,10 @@
 
 
 def kernel(
-    step_ref, normed_hbm, kg_hbm, master_hbm, moment1_hbm, moment2_hbm, anchor_hbm, momentum_hbm,
+    step_hbm, normed_hbm, kg_hbm, master_hbm, moment1_hbm, moment2_hbm, anchor_hbm, momentum_hbm,
     keysv, igv, merged_ref, first_ref, second_ref, anchor_ref, momentum_ref,
     xv, kgv, mv, m1v, m2v, av, ov, delta, core_got, half_sum, z_got, half_got,
-    w, g, gnat, first_send, first_recv,
-    r1, r1x, r2, r2x, third, r3,
+    w, g, gnat, keys_sum, packed, r1, r1x, r2, r2x, third, r3_send, r3, step_ref,
     load_sem, o_send, o_got,
     f_send, f_got, a2_send, a2_got, a2x_send, a2x_got,
     a3_send, a3_got, a3x_send, a3x_got,
@@ -63,14 +62,15 @@
     pair_dev = ((rep + 2) % 4, shard)
 
     pending = []
-
-    def send(src, dst, ssem, rsem, target):
+    pending_sums = []
+
+    def send(src, dst, ssem, rsem, target, queue=pending):
         copy = pltpu.make_async_remote_copy(
             src_ref=src, dst_ref=dst, send_sem=ssem, recv_sem=rsem,
             device_id=target, device_id_type=MESH,
         )
         copy.start()
-        pending.append(copy)
+        queue.append(copy)
 
     def got(dst, ssem, rsem):
         pltpu.make_async_remote_copy(
@@ -86,6 +86,7 @@
         pltpu.make_async_copy(moment1_hbm, m1v, load_sem.at[4]),
         pltpu.make_async_copy(moment2_hbm, m2v, load_sem.at[5]),
         pltpu.make_async_copy(momentum_hbm, ov, load_sem.at[6]),
+        pltpu.make_async_copy(step_hbm, step_ref, load_sem.at[7]),
     ]
     for copy in loads:
         copy.start()
@@ -96,15 +97,37 @@
         pl.semaphore_signal(barrier, inc=1, device_id=peer, device_id_type=MESH)
     pl.semaphore_wait(barrier, len(peers))
 
+    def pack_rows(v):
+        return jnp.concatenate([v[:, :HALF // 2], v[:, HALF // 2:]], axis=0).astype(BF16)
+
+    def unpack_rows(v):
+        v = f32(v)
+        return jnp.concatenate([v[:ROWS], v[ROWS:]], axis=1)
+
+    def piece_at(s, dz, d):
+        return packed.at[s, (z + dz) % 4, (first_pos[s] - d) % 4]
+
+    def send_second(s, d):
+        here = piece_at(s, 0, d)
+        for way, dz in ((0, 1), (1, 3)):
+            send(here, here, a2_send.at[s, way, d], a2_got.at[s, way, d], z_dev(dz))
+
+    def wait_second(s, way, d):
+        got(piece_at(s, 3 if way == 0 else 1, d), a2_send.at[s, way, d], a2_got.at[s, way, d])
+
+    def hand_second(s, d):
+        way = 0 if d in (0, 2) else 1
+        wait_second(s, way, d)
+        here = piece_at(s, 3 if way == 0 else 1, d)
+        send(here, here, a2x_send.at[s, d], a2x_got.at[s, d], z_dev(1 if way == 0 else 3))
+
     loads[0].wait()
     for s in (0, 1):
-        own = mv[:, s * HALF:(s + 1) * HALF]
-        packed = jnp.concatenate([own[:, :HALF // 2], own[:, HALF // 2:]], axis=0).astype(BF16)
-        first_send[s] = packed
-        first_recv[s, first_pos[s]] = packed
+        here = piece_at(s, 0, 0)
+        here[...] = pack_rows(mv[:, s * HALF:(s + 1) * HALF])
         for d in (1, 3, 2):
-            send(first_send.at[s], first_recv.at[s, first_pos[s]],
-                 f_send.at[s, d], f_got.at[s, d], first_dev[s](d))
+            send(here, here, f_send.at[s, d], f_got.at[s, d], first_dev[s](d))
+        send_second(s, 0)
 
     loads[3].wait()
     delta[...] = av[...] - mv[...]
@@ -116,14 +139,14 @@
     def send_relay(s):
         for n, k in enumerate(TO_RIGHT):
             send(g.at[s, chunk_at(s, 2, k)], r1x.at[s, 0, n],
-                 s1x_send.at[s, 0, n], s1x_got.at[s, 0, n], last_dev[s](1))
+                 s1x_send.at[s, 0, n], s1x_got.at[s, 0, n], last_dev[s](1), pending_sums)
         for n, k in enumerate(TO_LEFT):
             send(g.at[s, chunk_at(s, 2, k)], r1x.at[s, 1, n],
-                 s1x_send.at[s, 1, n], s1x_got.at[s, 1, n], last_dev[s](3))
+                 s1x_send.at[s, 1, n], s1x_got.at[s, 1, n], last_dev[s](3), pending_sums)
 
     def send_one(s, way, k):
         send(g.at[s, chunk_at(s, 1 if way == 0 else 3, k)], r1.at[s, way, k],
-             s1_send.at[s, way, k], s1_got.at[s, way, k], last_dev[s](1 if way == 0 else 3))
+             s1_send.at[s, way, k], s1_got.at[s, way, k], last_dev[s](1 if way == 0 else 3), pending_sums)
 
     loads[1].wait()
     loads[2].wait()
@@ -131,30 +154,18 @@
     def tn(lhs, rhs):
         return lax.dot_general(lhs, rhs, (((0,), (0,)), ((), ())), preferred_element_type=F32)
 
-    def grad_one(block):
+    def grad_block(block):
         def step(i, _):
             at = pl.multiple_of(block * BLOCK + i * TOK, 128)
-            part = tn(xv[:, pl.ds(at, TOK)], kgv[:, HALF:]).astype(BF16)
+            part = tn(xv[:, pl.ds(at, TOK)], kgv[...])
+            gnat[pl.ds(at, TOK)] = part[:, :HALF]
             flat = g.at[1, pl.ds(block * 4, 4)]
             for n in range(TOK // 96):
                 row = i * TOK + n * 96
-                flat[row // CHUNK, pl.ds(pl.multiple_of(row % CHUNK, 96), 96)] = part[n * 96:(n + 1) * 96]
+                rows = pl.ds(pl.multiple_of(row % CHUNK, 96), 96)
+                flat[row // CHUNK, rows] = part[n * 96:(n + 1) * 96, HALF:].astype(BF16)
             return 0
         lax.fori_loop(0, BLOCK // TOK, step, 0)
-
-    grad_one((x + 2) % 4)
-    send_relay(1)
-
-    got(core_got, o_send.at[0], o_got.at[0])
-    mine = pl.ds(pl.multiple_of(core * HALF, 128), HALF)
-    half_sum[...] = delta[:, mine] + core_got[:, mine]
-    send(half_sum, z_got, o_send.at[1], o_got.at[1], pair_dev)
-
-    def grad_zero(i, _):
-        at = pl.multiple_of(i * TOK, 128)
-        gnat[pl.ds(at, TOK)] = tn(xv[:, pl.ds(at, TOK)], kgv[:, :HALF])
-        return 0
-    lax.fori_loop(0, D // TOK, grad_zero, 0)
 
     def pack(block):
         def step(k, _):
@@ -167,35 +178,36 @@
             return 0
         lax.fori_loop(0, 4, step, 0)
 
+    grad_block((x + 2) % 4)
+    send_relay(1)
+
+    got(core_got, o_send.at[0], o_got.at[0])
+    mine = pl.ds(pl.multiple_of(core * HALF, 128), HALF)
+    half_sum[...] = delta[:, mine] + core_got[:, mine]
+    send(half_sum, z_got, o_send.at[1], o_got.at[1], pair_dev)
+
+    for d in (1, 3):
+        grad_block((x + d) % 4)
+        for k in (TO_LEFT if d == 1 else TO_RIGHT):
+            send_one(1, 0 if d == 1 else 1, k)
+    grad_block(x)
     pack((y + 2) % 4)
     send_relay(0)
+
+    for d in (1, 3, 2):
+        for s in (0, 1):
+            got(piece_at(s, 0, d), f_send.at[s, d], f_got.at[s, d])
+            send_second(s, d)
+
     for d in (1, 3):
-        grad_one((x + d) % 4)
         pack((y + d) % 4)
-        for s in (1, 0):
-            way = 0 if d == 1 else 1
-            for k in (TO_LEFT if d == 1 else TO_RIGHT):
-                send_one(s, way, k)
-    grad_one(x)
+        for k in (TO_LEFT if d == 1 else TO_RIGHT):
+            send_one(0, 0 if d == 1 else 1, k)
     pack(y)
 
-    def send_second(s, way, h):
-        here = w.at[s, last_pos[s] * 4 + z, pl.ds(h * HROWS, HROWS)]
-        send(here, here, a2_send.at[s, way, h], a2_got.at[s, way, h], z_dev(1 if way == 0 else 3))
-
-    for s in (0, 1):
-        for d in (1, 3, 2):
-            got(first_recv.at[s, (first_pos[s] - d) % 4], f_send.at[s, d], f_got.at[s, d])
-        pieces = []
-        for j in range(4):
-            piece = f32(first_recv[s, j])
-            pieces.append(jnp.concatenate([piece[:ROWS], piece[ROWS:]], axis=1))
-        w[s, last_pos[s] * 4 + z] = jnp.concatenate(pieces, axis=0).astype(BF16)
-        send_second(s, 0, 0)
-        send_second(s, 1, 1)
-    for s in (0, 1):
-        send_second(s, 0, 1)
-        send_second(s, 1, 0)
+    def assemble(s, k):
+        pieces = [unpack_rows(packed[s, (z + k) % 4, j]) for j in range(4)]
+        w[s, chunk_at(s, 0, k)] = jnp.concatenate(pieces, axis=0).astype(BF16)
 
     def add_rows(dst, rows, sources):
         def step(i, _):
@@ -215,23 +227,17 @@
                 add_rows(here, CHUNK, [here, r1x.at[s, way, n]])
                 send_one(s, way, k)
 
-    def second_at(s, d, h):
-        return w.at[s, last_pos[s] * 4 + (z + d) % 4, pl.ds(h * HROWS, HROWS)]
-
-    def wait_second(s, way, h):
-        got(second_at(s, 3 if way == 0 else 1, h), a2_send.at[s, way, h], a2_got.at[s, way, h])
-
     got(z_got, o_send.at[1], o_got.at[1])
     z_got[...] = half_sum[...] + z_got[...]
     send(z_got, half_got.at[:, mine], o_send.at[2], o_got.at[2], core_dev)
 
     hand_on(0)
-    for s in (0, 1):
-        for way in (0, 1):
-            wait_second(s, way, way)
-            here = second_at(s, 3 if way == 0 else 1, way)
-            send(here, here, a2x_send.at[s, way], a2x_got.at[s, way], z_dev(1 if way == 0 else 3))
+    for d in (0, 1, 3):
+        for s in (0, 1):
+            hand_second(s, d)
     hand_on(1)
+    for s in (0, 1):
+        hand_second(s, 2)
 
     def close(s, k, h, extra=()):
         rows = pl.ds(h * HROWS, HROWS)
@@ -248,7 +254,7 @@
     for s in (0, 1):
         for way in (0, 1):
             send(close(s, 2, way), r2x.at[s, way], s2x_send.at[s, way], s2x_got.at[s, way],
-                 z_dev(1 if way == 0 else 3))
+                 z_dev(1 if way == 0 else 3), pending_sums)
 
     def send_third(s, way, k):
         here = w.at[s, chunk_at(s, 0, k)]
@@ -260,13 +266,14 @@
         send(here, here, a3x_send.at[s, k], a3x_got.at[s, k], last_dev[s](1 if way == 0 else 3))
 
     for s in (0, 1):
+        assemble(s, 0)
         for way in (0, 1):
             send_third(s, way, 0)
 
     def send_plain_z(s, way):
         k, h = (1, 1) if way == 0 else (3, 0)
         send(close(s, k, h), r2.at[s, way, h], s2_send.at[s, way, h], s2_got.at[s, way, h],
-             z_dev(1 if way == 0 else 3))
+             z_dev(1 if way == 0 else 3), pending_sums)
 
     wait_last(1)
     for s in (0, 1):
@@ -276,30 +283,61 @@
         send_plain_z(s, 1)
 
     for s in (0, 1):
-        for way in (0, 1):
-            wait_second(s, way, 1 - way)
-    for k in (1, 3):
-        for s in (0, 1):
-            for way in (0, 1):
-                send_third(s, way, k)
-    for s in (0, 1):
-        for way in (0, 1):
-            got(second_at(s, 2, way), a2x_send.at[s, way], a2x_got.at[s, way])
-    for s in (0, 1):
-        for way in (0, 1):
-            send_third(s, way, 2)
+        for d in range(4):
+            wait_second(s, 1 if d in (0, 2) else 0, d)
+        for k in (1, 3):
+            assemble(s, k)
+        send_third(s, 0, 1)
+        send_third(s, 1, 1)
+        send_third(s, 1, 3)
+    for s in (0, 1):
+        for d in range(4):
+            got(piece_at(s, 2, d), a2x_send.at[s, d], a2x_got.at[s, d])
+        assemble(s, 2)
+        send_third(s, 0, 2)
+        send_third(s, 0, 3)
+        send_third(s, 1, 2)
 
     for s in (0, 1):
         for way in (0, 1):
             got(r2x.at[s, way], s2x_send.at[s, way], s2x_got.at[s, way])
             k, h = (1, 0) if way == 0 else (3, 1)
             send(close(s, k, h, (r2x.at[s, way],)), r2.at[s, way, h],
-                 s2_send.at[s, way, h], s2_got.at[s, way, h], z_dev(1 if way == 0 else 3))
-
-    for n in (1, 0):
+                 s2_send.at[s, way, h], s2_got.at[s, way, h], z_dev(1 if way == 0 else 3), pending_sums)
+
+    def nt(lhs, rhs):
+        return lax.dot_general(lhs, rhs, (((1,), (1,)), ((), ())), preferred_element_type=F32)
+
+    def weight(ref, b):
+        return ref[pl.ds(b * 4, 4)].reshape(BLOCK, HALF)
+
+    def multiply_one(d):
+        b = (x + d) % 4
+        block = weight(w.at[1], b)
+        at = pl.multiple_of(b * BLOCK, 128)
+        part = jnp.dot(xv[:, pl.ds(at, BLOCK)], block, preferred_element_type=F32)
+        if d == 0:
+            keys_sum[...] = part
+        else:
+            keys_sum[...] += part
+        for n in range(BLOCK // TOK):
+            rows = pl.ds(pl.multiple_of(b * BLOCK + n * TOK, 128), TOK)
+            gnat[rows, :TOK] = nt(kgv[:, HALF:], block[n * TOK:(n + 1) * TOK])
+
+    multiply_one(0)
+
+    for way, k in ((0, 0), (1, 1), (1, 3), (0, 2)):
         for s in (0, 1):
-            hand_third(s, 0, TO_RIGHT[n])
-            hand_third(s, 1, TO_LEFT[1 - n])
+            hand_third(s, way, k)
+
+    def wait_third(s, way):
+        for k in (TO_LEFT if way == 0 else TO_RIGHT):
+            got(w.at[s, chunk_at(s, 3 if way == 0 else 1, k)], a3_send.at[s, way, k], a3_got.at[s, way, k])
+
+    wait_third(1, 0)
+    multiply_one(3)
+    wait_third(1, 1)
+    multiply_one(1)
 
     wait_last(0)
     for s in (0, 1):
@@ -310,20 +348,19 @@
             add_rows(third.at[s, rows], HROWS,
                      [g.at[s, chunk_at(s, 0, 0), rows], r1.at[s, 0, 0, rows], r1.at[s, 1, 0, rows],
                       r2.at[s, 0, h], r2.at[s, 1, h]])
+        for j in range(4):
+            r3_send[s, j] = pack_rows(third[s, j * ROWS:(j + 1) * ROWS])
         for d in (2, 1, 3):
-            at = pl.multiple_of(((first_pos[s] + d) % 4) * ROWS, 8)
-            send(third.at[s, pl.ds(at, ROWS)], r3.at[s, d], s3_send.at[s, d], s3_got.at[s, d], first_dev[s](d))
-
-    for s in (0, 1):
-        for way, ks in ((0, TO_LEFT), (1, TO_RIGHT)):
-            for k in ks:
-                got(w.at[s, chunk_at(s, 3 if way == 0 else 1, k)], a3_send.at[s, way, k], a3_got.at[s, way, k])
+            send(r3_send.at[s, (first_pos[s] + d) % 4], r3.at[s, d], s3_send.at[s, d], s3_got.at[s, d], first_dev[s](d))
+
+    wait_third(0, 0)
+    wait_third(0, 1)
+    for s in (0, 1):
         for k in range(4):
             got(w.at[s, chunk_at(s, 2, k)], a3x_send.at[s, k], a3x_got.at[s, k])
 
-    for copy in pending:
+    for copy in pending_sums:
         copy.wait_send()
-    pending.clear()
     wnat = g.at[0]
 
     def unpack(k, _):
@@ -339,25 +376,21 @@
     lax.fori_loop(0, 4, unpack, 0)
 
     scale = D ** (-0.5)
-
-    def nt(lhs, rhs):
-        return lax.dot_general(lhs, rhs, (((1,), (1,)), ((), ())), preferred_element_type=F32)
-
-    def weight(ref, b):
-        return ref[pl.ds(b * 4, 4)].reshape(BLOCK, HALF)
-
-    def back(b, _):
-        at = pl.multiple_of(b * BLOCK, 128)
-        part = nt(kgv[:, :HALF], weight(wnat, b)) + nt(kgv[:, HALF:], weight(w.at[1], b))
-        igv[:, pl.ds(at, BLOCK)] = (part * scale).astype(BF16)
+    multiply_one(2)
+    keysv[:, HALF:] = (keys_sum[...] * scale).astype(BF16)
+
+    def multiply_zero(b, _):
+        block = weight(wnat, b)
+        part = jnp.dot(xv[:, pl.ds(pl.multiple_of(b * BLOCK, 128), BLOCK)], block, preferred_element_type=F32)
+        keys_sum[...] += part
+        for n in range(BLOCK // TOK):
+            at = pl.ds(pl.multiple_of(b * BLOCK + n * TOK, 128), TOK)
+            part = gnat[at, :TOK] + nt(kgv[:, :HALF], block[n * TOK:(n + 1) * TOK])
+            igv[:, at] = (part * scale).astype(BF16)
         return 0
-    lax.fori_loop(0, 4, back, 0)
-    for s, ref in ((0, wnat), (1, w.at[1])):
-        total = None
-        for b in range(4):
-            part = jnp.dot(xv[:, b * BLOCK:(b + 1) * BLOCK], weight(ref, b), preferred_element_type=F32)
-            total = part if total is None else total + part
-        keysv[:, s * HALF:(s + 1) * HALF] = (total * scale).astype(BF16)
+    keys_sum[...] = jnp.zeros_like(keys_sum)
+    lax.fori_loop(0, 4, multiply_zero, 0)
+    keysv[:, :HALF] = (keys_sum[...] * scale).astype(BF16)
 
     for copy in loads[4:]:
         copy.wait()
@@ -378,7 +411,7 @@
         total = third[s, pl.ds(at, ROWS)]
         for d in (1, 3, 2):
             got(r3.at[s, d], s3_send.at[s, d], s3_got.at[s, d])
-            total = total + r3[s, d]
+            total = total + unpack_rows(r3[s, d])
         gradient = total * scale
         cols = slice(s * HALF, (s + 1) * HALF)
         first_new = beta_first * m1v[:, cols] + (1.0 - beta_first) * gradient
@@ -403,7 +436,7 @@
             pltpu.VMEM((TOK, KD), BF16),
             pltpu.VMEM((TOK, D), BF16),
         ) + (pltpu.VMEM(rows, F32),) * 5,
-        in_specs=[pl.BlockSpec(memory_space=pltpu.SMEM)] + [pl.BlockSpec(memory_space=pl.ANY)] * 7,
+        in_specs=[pl.BlockSpec(memory_space=pl.ANY)] * 8,
         out_specs=(pl.BlockSpec(memory_space=pltpu.VMEM),) * 7,
         scratch_shapes=[
             pltpu.VMEM((TOK, D), BF16),
@@ -421,23 +454,25 @@
             pltpu.VMEM((2, 16, CHUNK, HALF), BF16),
             pltpu.VMEM((2, 16, CHUNK, HALF), BF16),
             pltpu.VMEM((D, HALF), F32),
-            pltpu.VMEM((2, 2 * ROWS, HALF // 2), BF16),
-            pltpu.VMEM((2, 4, 2 * ROWS, HALF // 2), BF16),
+            pltpu.VMEM((TOK, HALF), F32),
+            pltpu.VMEM((2, 4, 4, 2 * ROWS, HALF // 2), BF16),
             pltpu.VMEM((2, 2, 4, CHUNK, HALF), BF16),
             pltpu.VMEM((2, 2, 2, CHUNK, HALF), BF16),
             pltpu.VMEM((2, 2, 2, HROWS, HALF), BF16),
             pltpu.VMEM((2, 2, HROWS, HALF), BF16),
             pltpu.VMEM((2, CHUNK, HALF), F32),
-            pltpu.VMEM((2, 4, ROWS, HALF), F32),
-            dma((7,)), dma((3,)), dma((3,)),
+            pltpu.VMEM((2, 4, 2 * ROWS, HALF // 2), BF16),
+            pltpu.VMEM((2, 4, 2 * ROWS, HALF // 2), BF16),
+            pltpu.SMEM((1,), jnp.int32),
+            dma((8,)), dma((3,)), dma((3,)),
             dma((2, 4)), dma((2, 4)),
-            dma((2, 2, 2)), dma((2, 2, 2)), dma((2, 2)), dma((2, 2)),
+            dma((2, 2, 4)), dma((2, 2, 4)), dma((2, 4)), dma((2, 4)),
             dma((2, 2, 4)), dma((2, 2, 4)), dma((2, 4)), dma((2, 4)),
             dma((2, 2, 2)), dma((2, 2, 2)), dma((2, 2, 4)), dma((2, 2, 4)),
             dma((2, 2)), dma((2, 2)), dma((2, 2, 2)), dma((2, 2, 2)), dma((2, 4)), dma((2, 4)),
         ],
         compiler_params=pltpu.CompilerParams(
-            collective_id=0, has_side_effects=True, vmem_limit_bytes=48 * 2**20
+            collective_id=0, has_side_effects=True, vmem_limit_bytes=56 * 2**20
         ),
         cost_estimate=pl.CostEstimate(
             flops=6 * TOK * D * KD, bytes_accessed=10 * 2**20, transcendentals=0

time: 121 us -> 109 us (0.901)
  Pallas kernels: 118 us -> 108 us
    pallas_call x1, Pallas kernels: 116 us -> 105 us  [exchange(): pl.pallas_call(kernel, out_shape=(pltpu.VMEM((TOK, KD), BF16), pltpu.VMEM...]
where the time goes in v3:
time: 109 us
  Pallas kernels  108 us (99%)
  between operations  1.29 us (1%)
    pallas_call x1, Pallas kernels, exchange(): pl.pallas_call(kernel, out_shape=(pltpu.VMEM((TOK, KD), BF16), pltpu.VMEM...  105 us
    pallas_call x1, Pallas kernels, store(): pl.pallas_call(store_kernel, out_shape=tuple((jax.ShapeDtypeStruct(a.shap...  2.56 us

profile of v3, /device:TPU:6, one launch (start us, length us, event | category | flops | bytes accessed | tf_op | source)
XLA Modules:
  0.0 108.9 jit_solution(13409557820178668377)
XLA Ops:
  1.3 105.0 %exchange.1 = (bf16[384,1024]{1,0:T(8,128)(2,1)S(1)}, bf16[384,4608]{1,0:T(8,128)(2,1)S(1)}, f32[72,1024]{1,0:T(8,128)S(1)}, f32[72,1024]{1,0:T(8,128)S(1)}, f32...) custom-call(s32[1]{0:T(128)S(6)} %copy.15.step_hbm, bf16[384,4608]{1,0:T(8,128)(2,1)} %normed_hbm.1, ...), custom_call_target="tpu_custom_call" | custom-call | flops 10871635968 | bytes 10485760 | tf_op jit(solution)/shard_map/exchange/pallas_call | solution.py:433
  106.3 2.6 %store.1 = (bf16[384,1024]{1,0:T(8,128)(2,1)}, bf16[384,4608]{1,0:T(8,128)(2,1)}, f32[72,1024]{1,0:T(8,128)}, f32[72,1024]{1,0:T(8,128)}, f32[72,1024]{1,0:T(8,1...) custom-call(bf16[384,1024]{1,0:T(8,128)(2,1)S(1)} %get-tuple-element.21.refs_0_, ...), custom_call_target="tpu_custom_call" | custom-call | tf_op jit(solution)/shard_map/store/pallas_call | solution.py:495

commit v4 on v3

--- a/solution.py
+++ b/solution.py
@@ -62,15 +62,15 @@
     pair_dev = ((rep + 2) % 4, shard)
 
     pending = []
-    pending_sums = []
-
-    def send(src, dst, ssem, rsem, target, queue=pending):
+    pending_gather = []
+
+    def send(src, dst, ssem, rsem, target, queue=None):
         copy = pltpu.make_async_remote_copy(
             src_ref=src, dst_ref=dst, send_sem=ssem, recv_sem=rsem,
             device_id=target, device_id_type=MESH,
         )
         copy.start()
-        queue.append(copy)
+        (pending if queue is None else queue).append(copy)
 
     def got(dst, ssem, rsem):
         pltpu.make_async_remote_copy(
@@ -136,17 +136,17 @@
     def chunk_at(s, d, k):
         return ((last_pos[s] + d) % 4) * 4 + (z + k) % 4
 
-    def send_relay(s):
-        for n, k in enumerate(TO_RIGHT):
-            send(g.at[s, chunk_at(s, 2, k)], r1x.at[s, 0, n],
-                 s1x_send.at[s, 0, n], s1x_got.at[s, 0, n], last_dev[s](1), pending_sums)
-        for n, k in enumerate(TO_LEFT):
-            send(g.at[s, chunk_at(s, 2, k)], r1x.at[s, 1, n],
-                 s1x_send.at[s, 1, n], s1x_got.at[s, 1, n], last_dev[s](3), pending_sums)
+    def send_relay(s, part, at):
+        rows = pl.ds(pl.multiple_of(at, HROWS), HROWS)
+        for way, ks in ((0, TO_RIGHT), (1, TO_LEFT)):
+            for n, k in enumerate(ks):
+                send(g.at[s, chunk_at(s, 2, k), rows], r1x.at[s, way, n, rows],
+                     s1x_send.at[s, way, n, part], s1x_got.at[s, way, n, part],
+                     last_dev[s](1 if way == 0 else 3))
 
     def send_one(s, way, k):
         send(g.at[s, chunk_at(s, 1 if way == 0 else 3, k)], r1.at[s, way, k],
-             s1_send.at[s, way, k], s1_got.at[s, way, k], last_dev[s](1 if way == 0 else 3), pending_sums)
+             s1_send.at[s, way, k], s1_got.at[s, way, k], last_dev[s](1 if way == 0 else 3))
 
     loads[1].wait()
     loads[2].wait()
@@ -167,43 +167,49 @@
             return 0
         lax.fori_loop(0, BLOCK // TOK, step, 0)
 
-    def pack(block):
+    def pack(block, pair):
         def step(k, _):
-            for half in (0, 1):
-                pieces = [
-                    gnat[pl.ds(pl.multiple_of(a * BLOCK + k * CHUNK + block * ROWS, 8), ROWS)]
-                    for a in (2 * half, 2 * half + 1)
-                ]
-                g[0, block * 4 + k, half * HROWS:(half + 1) * HROWS] = jnp.concatenate(pieces, axis=0).astype(BF16)
+            pieces = [
+                gnat[pl.ds(pl.multiple_of((2 * pair + a) * BLOCK + k * CHUNK + block * ROWS, 8), ROWS)]
+                for a in (0, 1)
+            ]
+            rows = pl.ds(pl.multiple_of(pair * HROWS, HROWS), HROWS)
+            g[0, block * 4 + k, rows] = jnp.concatenate(pieces, axis=0).astype(BF16)
             return 0
         lax.fori_loop(0, 4, step, 0)
 
-    grad_block((x + 2) % 4)
-    send_relay(1)
+    opposite = (x + 2) % 4
+    pairs = (opposite // 2, 1 - opposite // 2)
+    grad_block(opposite)
+    for part in (0, 1):
+        send_relay(1, part, part * HROWS)
 
     got(core_got, o_send.at[0], o_got.at[0])
     mine = pl.ds(pl.multiple_of(core * HALF, 128), HALF)
     half_sum[...] = delta[:, mine] + core_got[:, mine]
     send(half_sum, z_got, o_send.at[1], o_got.at[1], pair_dev)
 
-    for d in (1, 3):
-        grad_block((x + d) % 4)
-        for k in (TO_LEFT if d == 1 else TO_RIGHT):
-            send_one(1, 0 if d == 1 else 1, k)
-    grad_block(x)
-    pack((y + 2) % 4)
-    send_relay(0)
+    grad_block(opposite + 1 - 2 * (opposite % 2))
+    pack((y + 2) % 4, pairs[0])
+    send_relay(0, 0, pairs[0] * HROWS)
 
     for d in (1, 3, 2):
         for s in (0, 1):
             got(piece_at(s, 0, d), f_send.at[s, d], f_got.at[s, d])
             send_second(s, d)
 
+    grad_block(x)
+    grad_block(x + 1 - 2 * (x % 2))
+    pack((y + 2) % 4, pairs[1])
+    send_relay(0, 1, pairs[1] * HROWS)
     for d in (1, 3):
-        pack((y + d) % 4)
-        for k in (TO_LEFT if d == 1 else TO_RIGHT):
-            send_one(0, 0 if d == 1 else 1, k)
-    pack(y)
+        for pair in (0, 1):
+            pack((y + d) % 4, pair)
+        for s in (1, 0):
+            for k in (TO_LEFT if d == 1 else TO_RIGHT):
+                send_one(s, 0 if d == 1 else 1, k)
+    for pair in (0, 1):
+        pack(y, pair)
 
     def assemble(s, k):
         pieces = [unpack_rows(packed[s, (z + k) % 4, j]) for j in range(4)]
@@ -222,7 +228,10 @@
     def hand_on(n):
         for s in (1, 0):
             for way, k in ((0, TO_RIGHT[n]), (1, TO_LEFT[n])):
-                got(r1x.at[s, way, n], s1x_send.at[s, way, n], s1x_got.at[s, way, n])
+                for part in (0, 1):
+                    at = (part if s == 1 else pairs[part]) * HROWS
+                    got(r1x.at[s, way, n, pl.ds(pl.multiple_of(at, HROWS), HROWS)],
+                        s1x_send.at[s, way, n, part], s1x_got.at[s, way, n, part])
                 here = g.at[s, chunk_at(s, 1 if way == 0 else 3, k)]
                 add_rows(here, CHUNK, [here, r1x.at[s, way, n]])
                 send_one(s, way, k)
@@ -254,16 +263,16 @@
     for s in (0, 1):
         for way in (0, 1):
             send(close(s, 2, way), r2x.at[s, way], s2x_send.at[s, way], s2x_got.at[s, way],
-                 z_dev(1 if way == 0 else 3), pending_sums)
+                 z_dev(1 if way == 0 else 3))
 
     def send_third(s, way, k):
         here = w.at[s, chunk_at(s, 0, k)]
-        send(here, here, a3_send.at[s, way, k], a3_got.at[s, way, k], last_dev[s](1 if way == 0 else 3))
+        send(here, here, a3_send.at[s, way, k], a3_got.at[s, way, k], last_dev[s](1 if way == 0 else 3), pending_gather)
 
     def hand_third(s, way, k):
         here = w.at[s, chunk_at(s, 3 if way == 0 else 1, k)]
         got(here, a3_send.at[s, way, k], a3_got.at[s, way, k])
-        send(here, here, a3x_send.at[s, k], a3x_got.at[s, k], last_dev[s](1 if way == 0 else 3))
+        send(here, here, a3x_send.at[s, k], a3x_got.at[s, k], last_dev[s](1 if way == 0 else 3), pending_gather)
 
     for s in (0, 1):
         assemble(s, 0)
@@ -273,7 +282,7 @@
     def send_plain_z(s, way):
         k, h = (1, 1) if way == 0 else (3, 0)
         send(close(s, k, h), r2.at[s, way, h], s2_send.at[s, way, h], s2_got.at[s, way, h],
-             z_dev(1 if way == 0 else 3), pending_sums)
+             z_dev(1 if way == 0 else 3))
 
     wait_last(1)
     for s in (0, 1):
@@ -303,7 +312,7 @@
             got(r2x.at[s, way], s2x_send.at[s, way], s2x_got.at[s, way])
             k, h = (1, 0) if way == 0 else (3, 1)
             send(close(s, k, h, (r2x.at[s, way],)), r2.at[s, way, h],
-                 s2_send.at[s, way, h], s2_got.at[s, way, h], z_dev(1 if way == 0 else 3), pending_sums)
+                 s2_send.at[s, way, h], s2_got.at[s, way, h], z_dev(1 if way == 0 else 3))
 
     def nt(lhs, rhs):
         return lax.dot_general(lhs, rhs, (((1,), (1,)), ((), ())), preferred_element_type=F32)
@@ -359,28 +368,25 @@
         for k in range(4):
             got(w.at[s, chunk_at(s, 2, k)], a3x_send.at[s, k], a3x_got.at[s, k])
 
-    for copy in pending_sums:
+    for copy in pending_gather:
         copy.wait_send()
-    wnat = g.at[0]
-
-    def unpack(k, _):
+
+    def unpack(i, _):
+        k = i // 4
+        cols = pl.ds(pl.multiple_of(i % 4 * 128, 128), 128)
+        chunks = [f32(w[0, b * 4 + k, :, cols]) for b in range(4)]
         for a in range(4):
-            low = a * ROWS - 8 * (a % 2)
-            pieces = []
-            for b in range(4):
-                piece = f32(w[0, b * 4 + k, low:low + ROWS + 8])
-                skip = 8 * (a % 2)
-                pieces.append(piece[skip:skip + ROWS])
-            wnat[a * 4 + k] = jnp.concatenate(pieces, axis=0).astype(BF16)
+            rows = [chunk[a * ROWS:(a + 1) * ROWS] for chunk in chunks]
+            w[0, a * 4 + k, :, cols] = jnp.concatenate(rows, axis=0).astype(BF16)
         return 0
-    lax.fori_loop(0, 4, unpack, 0)
+    lax.fori_loop(0, 16, unpack, 0)
 
     scale = D ** (-0.5)
     multiply_one(2)
     keysv[:, HALF:] = (keys_sum[...] * scale).astype(BF16)
 
     def multiply_zero(b, _):
-        block = weight(wnat, b)
+        block = weight(w.at[0], b)
         part = jnp.dot(xv[:, pl.ds(pl.multiple_of(b * BLOCK, 128), BLOCK)], block, preferred_element_type=F32)
         keys_sum[...] += part
         for n in range(BLOCK // TOK):
@@ -468,7 +474,7 @@
             dma((2, 4)), dma((2, 4)),
             dma((2, 2, 4)), dma((2, 2, 4)), dma((2, 4)), dma((2, 4)),
             dma((2, 2, 4)), dma((2, 2, 4)), dma((2, 4)), dma((2, 4)),
-            dma((2, 2, 2)), dma((2, 2, 2)), dma((2, 2, 4)), dma((2, 2, 4)),
+            dma((2, 2, 2, 2)), dma((2, 2, 2, 2)), dma((2, 2, 4)), dma((2, 2, 4)),
             dma((2, 2)), dma((2, 2)), dma((2, 2, 2)), dma((2, 2, 2)), dma((2, 4)), dma((2, 4)),
         ],
         compiler_params=pltpu.CompilerParams(

time: 109 us -> 107 us (0.982); the launches traced: 109 us -> 105 us
  Pallas kernels: 108 us -> 104 us
    pallas_call x1, Pallas kernels: 105 us -> 101 us  [exchange(): pl.pallas_call(kernel, out_shape=(pltpu.VMEM((TOK, KD), BF16), pltpu.VMEM...]
where the time goes in v4:
time: 107 us; the launch traced here: 105 us
  Pallas kernels  104 us (97%)
  between operations  1.29 us (1%)
    pallas_call x1, Pallas kernels, exchange(): pl.pallas_call(kernel, out_shape=(pltpu.VMEM((TOK, KD), BF16), pltpu.VMEM...  101 us
    pallas_call x1, Pallas kernels, store(): pl.pallas_call(store_kernel, out_shape=tuple((jax.ShapeDtypeStruct(a.shap...  2.56 us

profile of v4, /device:TPU:6, one launch (start us, length us, event | category | flops | bytes accessed | tf_op | source)
XLA Modules:
  0.0 105.2 jit_solution(12540020571323720380)
XLA Ops:
  1.3 101.4 %exchange.1 = (bf16[384,1024]{1,0:T(8,128)(2,1)S(1)}, bf16[384,4608]{1,0:T(8,128)(2,1)S(1)}, f32[72,1024]{1,0:T(8,128)S(1)}, f32[72,1024]{1,0:T(8,128)S(1)}, f32...) custom-call(s32[1]{0:T(128)S(6)} %copy.15.step_hbm, bf16[384,4608]{1,0:T(8,128)(2,1)} %normed_hbm.1, ...), custom_call_target="tpu_custom_call" | custom-call | flops 10871635968 | bytes 10485760 | tf_op jit(solution)/shard_map/exchange/pallas_call | solution.py:439
  102.7 2.6 %store.1 = (bf16[384,1024]{1,0:T(8,128)(2,1)}, bf16[384,4608]{1,0:T(8,128)(2,1)}, f32[72,1024]{1,0:T(8,128)}, f32[72,1024]{1,0:T(8,128)}, f32[72,1024]{1,0:T(8,1...) custom-call(bf16[384,1024]{1,0:T(8,128)(2,1)S(1)} %get-tuple-element.21.refs_0_, ...), custom_call_target="tpu_custom_call" | custom-call | tf_op jit(solution)/shard_map/store/pallas_call | solution.py:501

commit v5 on v4

--- a/solution.py
+++ b/solution.py
@@ -36,7 +36,7 @@
     step_hbm, normed_hbm, kg_hbm, master_hbm, moment1_hbm, moment2_hbm, anchor_hbm, momentum_hbm,
     keysv, igv, merged_ref, first_ref, second_ref, anchor_ref, momentum_ref,
     xv, kgv, mv, m1v, m2v, av, ov, delta, core_got, half_sum, z_got, half_got,
-    w, g, gnat, keys_sum, packed, r1, r1x, r2, r2x, third, r3_send, r3, step_ref,
+    w, g, gnat, keys_sum, keys_sum0, xp, packed, r1, r1x, r2, r2x, third, r3_send, r3, step_ref,
     load_sem, o_send, o_got,
     f_send, f_got, a2_send, a2_got, a2x_send, a2x_got,
     a3_send, a3_got, a3x_send, a3x_got,
@@ -211,6 +211,19 @@
     for pair in (0, 1):
         pack(y, pair)
 
+    def permute(i, _):
+        rows = pl.ds(pl.multiple_of(i * 32, 32), 32)
+        for b in range(4):
+            pieces = []
+            for k in range(4):
+                for a in range(4):
+                    at = a * BLOCK + k * CHUNK + b * ROWS
+                    pieces.append(xv[rows, at:at + ROWS])
+            xp[rows, b * BLOCK:(b + 1) * BLOCK] = jnp.concatenate(pieces, axis=1)
+        return 0
+
+    lax.fori_loop(0, 6, permute, 0)
+
     def assemble(s, k):
         pieces = [unpack_rows(packed[s, (z + k) % 4, j]) for j in range(4)]
         w[s, chunk_at(s, 0, k)] = jnp.concatenate(pieces, axis=0).astype(BF16)
@@ -259,6 +272,7 @@
             for way in (0, 1):
                 got(r1.at[s, way, k], s1_send.at[s, way, k], s1_got.at[s, way, k])
 
+    lax.fori_loop(6, TOK // 32, permute, 0)
     wait_last(2)
     for s in (0, 1):
         for way in (0, 1):
@@ -333,11 +347,22 @@
             rows = pl.ds(pl.multiple_of(b * BLOCK + n * TOK, 128), TOK)
             gnat[rows, :TOK] = nt(kgv[:, HALF:], block[n * TOK:(n + 1) * TOK])
 
-    multiply_one(0)
 
     for way, k in ((0, 0), (1, 1), (1, 3), (0, 2)):
         for s in (0, 1):
             hand_third(s, way, k)
+
+    def multiply_keys(d):
+        b = (y + d) % 4
+        at = pl.multiple_of(b * BLOCK, 128)
+        part = jnp.dot(xp[:, pl.ds(at, BLOCK)], weight(w.at[0], b), preferred_element_type=F32)
+        if d == 0:
+            keys_sum0[...] = part
+        else:
+            keys_sum0[...] += part
+
+    multiply_one(0)
+    multiply_keys(0)
 
     def wait_third(s, way):
         for k in (TO_LEFT if way == 0 else TO_RIGHT):
@@ -347,6 +372,10 @@
     multiply_one(3)
     wait_third(1, 1)
     multiply_one(1)
+    wait_third(0, 0)
+    multiply_keys(3)
+    wait_third(0, 1)
+    multiply_keys(1)
 
     wait_last(0)
     for s in (0, 1):
@@ -362,11 +391,12 @@
         for d in (2, 1, 3):
             send(r3_send.at[s, (first_pos[s] + d) % 4], r3.at[s, d], s3_send.at[s, d], s3_got.at[s, d], first_dev[s](d))
 
-    wait_third(0, 0)
-    wait_third(0, 1)
-    for s in (0, 1):
-        for k in range(4):
-            got(w.at[s, chunk_at(s, 2, k)], a3x_send.at[s, k], a3x_got.at[s, k])
+    for k in range(4):
+        got(w.at[1, chunk_at(1, 2, k)], a3x_send.at[1, k], a3x_got.at[1, k])
+    multiply_one(2)
+    for k in range(4):
+        got(w.at[0, chunk_at(0, 2, k)], a3x_send.at[0, k], a3x_got.at[0, k])
+    multiply_keys(2)
 
     for copy in pending_gather:
         copy.wait_send()
@@ -382,21 +412,17 @@
     lax.fori_loop(0, 16, unpack, 0)
 
     scale = D ** (-0.5)
-    multiply_one(2)
     keysv[:, HALF:] = (keys_sum[...] * scale).astype(BF16)
 
     def multiply_zero(b, _):
         block = weight(w.at[0], b)
-        part = jnp.dot(xv[:, pl.ds(pl.multiple_of(b * BLOCK, 128), BLOCK)], block, preferred_element_type=F32)
-        keys_sum[...] += part
         for n in range(BLOCK // TOK):
             at = pl.ds(pl.multiple_of(b * BLOCK + n * TOK, 128), TOK)
             part = gnat[at, :TOK] + nt(kgv[:, :HALF], block[n * TOK:(n + 1) * TOK])
             igv[:, at] = (part * scale).astype(BF16)
         return 0
-    keys_sum[...] = jnp.zeros_like(keys_sum)
     lax.fori_loop(0, 4, multiply_zero, 0)
-    keysv[:, :HALF] = (keys_sum[...] * scale).astype(BF16)
+    keysv[:, :HALF] = (keys_sum0[...] * scale).astype(BF16)
 
     for copy in loads[4:]:
         copy.wait()
@@ -461,6 +487,8 @@
             pltpu.VMEM((2, 16, CHUNK, HALF), BF16),
             pltpu.VMEM((D, HALF), F32),
             pltpu.VMEM((TOK, HALF), F32),
+            pltpu.VMEM((TOK, HALF), F32),
+            pltpu.VMEM((TOK, D), BF16),
             pltpu.VMEM((2, 4, 4, 2 * ROWS, HALF // 2), BF16),
             pltpu.VMEM((2, 2, 4, CHUNK, HALF), BF16),
             pltpu.VMEM((2, 2, 2, CHUNK, HALF), BF16),

time: 107 us -> 105 us (0.981)
  Pallas kernels: 104 us -> 102 us
    pallas_call x1, Pallas kernels: 101 us -> 99.7 us  [exchange(): pl.pallas_call(kernel, out_shape=(pltpu.VMEM((TOK, KD), BF16), pltpu.VMEM...]
where the time goes in v5:
time: 105 us; the launch traced here: 104 us
  Pallas kernels  102 us (97%)
  between operations  1.29 us (1%)
    pallas_call x1, Pallas kernels, exchange(): pl.pallas_call(kernel, out_shape=(pltpu.VMEM((TOK, KD), BF16), pltpu.VMEM...  99.7 us
    pallas_call x1, Pallas kernels, store(): pl.pallas_call(store_kernel, out_shape=tuple((jax.ShapeDtypeStruct(a.shap...  2.56 us

profile of v5, /device:TPU:6, one launch (start us, length us, event | category | flops | bytes accessed | tf_op | source)
XLA Modules:
  0.0 103.5 jit_solution(15694614335129284145)
XLA Ops:
  1.3 99.7 %exchange.1 = (bf16[384,1024]{1,0:T(8,128)(2,1)S(1)}, bf16[384,4608]{1,0:T(8,128)(2,1)S(1)}, f32[72,1024]{1,0:T(8,128)S(1)}, f32[72,1024]{1,0:T(8,128)S(1)}, f32...) custom-call(s32[1]{0:T(128)S(6)} %copy.15.step_hbm, bf16[384,4608]{1,0:T(8,128)(2,1)} %normed_hbm.1, ...), custom_call_target="tpu_custom_call" | custom-call | flops 10871635968 | bytes 10485760 | tf_op jit(solution)/shard_map/exchange/pallas_call | solution.py:465
  101.0 2.6 %store.1 = (bf16[384,1024]{1,0:T(8,128)(2,1)}, bf16[384,4608]{1,0:T(8,128)(2,1)}, f32[72,1024]{1,0:T(8,128)}, f32[72,1024]{1,0:T(8,128)}, f32[72,1024]{1,0:T(8,1...) custom-call(bf16[384,1024]{1,0:T(8,128)(2,1)S(1)} %get-tuple-element.21.refs_0_, ...), custom_call_target="tpu_custom_call" | custom-call | tf_op jit(solution)/shard_map/store/pallas_call | solution.py:529

commit v6 on v5

--- a/solution.py
+++ b/solution.py
@@ -377,6 +377,9 @@
     wait_third(0, 1)
     multiply_keys(1)
 
+    for k in range(4):
+        got(w.at[1, chunk_at(1, 2, k)], a3x_send.at[1, k], a3x_got.at[1, k])
+    multiply_one(2)
     wait_last(0)
     for s in (0, 1):
         for h in (0, 1):
@@ -391,9 +394,6 @@
         for d in (2, 1, 3):
             send(r3_send.at[s, (first_pos[s] + d) % 4], r3.at[s, d], s3_send.at[s, d], s3_got.at[s, d], first_dev[s](d))
 
-    for k in range(4):
-        got(w.at[1, chunk_at(1, 2, k)], a3x_send.at[1, k], a3x_got.at[1, k])
-    multiply_one(2)
     for k in range(4):
         got(w.at[0, chunk_at(0, 2, k)], a3x_send.at[0, k], a3x_got.at[0, k])
     multiply_keys(2)

time: 105 us -> 105 us (level)
  no operation moved by 1% of the time
where the time goes in v6:
time: 105 us; the launch traced here: 103 us
  Pallas kernels  102 us (97%)
  between operations  1.29 us (1%)
    pallas_call x1, Pallas kernels, exchange(): pl.pallas_call(kernel, out_shape=(pltpu.VMEM((TOK, KD), BF16), pltpu.VMEM...  99 us
    pallas_call x1, Pallas kernels, store(): pl.pallas_call(store_kernel, out_shape=tuple((jax.ShapeDtypeStruct(a.shap...  2.56 us

profile of v6, /device:TPU:6, one launch (start us, length us, event | category | flops | bytes accessed | tf_op | source)
XLA Modules:
  0.0 102.8 jit_solution(9737160636403162953)
XLA Ops:
  1.3 99.0 %exchange.1 = (bf16[384,1024]{1,0:T(8,128)(2,1)S(1)}, bf16[384,4608]{1,0:T(8,128)(2,1)S(1)}, f32[72,1024]{1,0:T(8,128)S(1)}, f32[72,1024]{1,0:T(8,128)S(1)}, f32...) custom-call(s32[1]{0:T(128)S(6)} %copy.15.step_hbm, bf16[384,4608]{1,0:T(8,128)(2,1)} %normed_hbm.1, ...), custom_call_target="tpu_custom_call" | custom-call | flops 10871635968 | bytes 10485760 | tf_op jit(solution)/shard_map/exchange/pallas_call | solution.py:465
  100.3 2.6 %store.1 = (bf16[384,1024]{1,0:T(8,128)(2,1)}, bf16[384,4608]{1,0:T(8,128)(2,1)}, f32[72,1024]{1,0:T(8,128)}, f32[72,1024]{1,0:T(8,128)}, f32[72,1024]{1,0:T(8,1...) custom-call(bf16[384,1024]{1,0:T(8,128)(2,1)S(1)} %get-tuple-element.21.refs_0_, ...), custom_call_target="tpu_custom_call" | custom-call | tf_op jit(solution)/shard_map/store/pallas_call | solution.py:529
